TPU v7x, 1024 devices: a whole 8x8x8 slice. The times are simulated.
1024 devices in a mesh: ctx: 64 (over x, y), head: 16 (over z, core).
Axes of the slice: x: 8, y: 8, z: 8, core: 2. Of those that a mesh axis runs over, the one named last changes fastest.
Arguments:
- queries: bfloat16 [12288, 64, 128], P(('ctx', 'head')), may hold values from -36 to 36
- keys: bfloat16 [131072, 16, 128], P('ctx', 'head'), may hold values from -5.5 to 5.5
- values: bfloat16 [131072, 16, 128], P('ctx', 'head'), may hold values from -6 to 6
- out_grad: bfloat16 [12288, 64, 128], P(('ctx', 'head')), may hold values from -192 to 192
- selected: int32 [16, 192, 16], P('head'), may hold values from 0 to 2047, as said below
Outputs:
- query_grad: bfloat16 [12288, 64, 128], P(('ctx', 'head'))
- key_grad: bfloat16 [131072, 16, 128], P('ctx', 'head')
- value_grad: bfloat16 [131072, 16, 128], P('ctx', 'head')
Inputs may be any that keep to these rules, and one draw needn't show every extreme that they name: The 16 blocks of one query block and group are distinct, and no block is selected twice by the query blocks of one index of ctx in one group. Key blocks j * 32 to (j + 1) * 32 - 1 are held by index j of ctx; the 3 query blocks of one index of ctx select at most 1 block held by any one index of ctx, for each group, and in each group some index of ctx has exactly 1 of its blocks selected by the query blocks of every index of ctx.
All inputs are finite; a program needn't handle non-finite values.
Results may differ from a plain program's by a relative error of at most 0.0049.
Values may be sent and summed in bfloat16 or wider, within the bound.
No kernel may reach another device: no remote copies, remote signals or barrier semaphores. Data moves between devices by JAX's collectives and lax.ppermute only.
A program may use at most 32 MiB of HBM per device.

v0:
```python
import jax
import jax.numpy as jnp
from jax import lax
from jax.sharding import PartitionSpec as P

BLOCK = 64
SELECTED = 16


def send_key_terms(placed):
    return lax.all_to_all(placed, "ctx", split_axis=0, concat_axis=0, tiled=True)


def send_value_terms(placed):
    return lax.all_to_all(placed, "ctx", split_axis=0, concat_axis=0, tiled=True)


def per_device(queries, keys, values, out_grad, selected):
    ctx_count = lax.axis_size("ctx")
    ctx_index = lax.axis_index("ctx")
    local_q, local_g = (
        lax.all_to_all(queries, "head", split_axis=1, concat_axis=0, tiled=True),
        lax.all_to_all(out_grad, "head", split_axis=1, concat_axis=0, tiled=True),
    )
    query_rows, group_heads, head_dim = local_q.shape
    block_count = query_rows // BLOCK
    wanted = block_count * SELECTED
    slot_count = (4 * wanted + 3 * ctx_count - 1) // (3 * ctx_count)
    owned = keys.shape[0] // BLOCK
    listing = selected[0].reshape(ctx_count, wanted)
    owners = listing // owned
    within = listing % owned
    position = jnp.arange(wanted, dtype=jnp.int32)
    before = position[None, :] < position[:, None]
    ranking = jnp.sum((owners[:, :, None] == owners[:, None, :]) & before[None], axis=2)
    slot_range = jnp.arange(slot_count, dtype=jnp.int32)
    matches = (owners == ctx_index)[:, :, None] & (ranking[:, :, None] == slot_range[None, None, :])
    send_rows = jnp.sum(jnp.where(matches, within[:, :, None], 0), axis=1)
    filled = jnp.any(matches, axis=1)
    key_tiles = keys[:, 0, :].reshape(owned, BLOCK, head_dim)
    value_tiles = values[:, 0, :].reshape(owned, BLOCK, head_dim)
    fetched_k, fetched_v = (
        lax.all_to_all(key_tiles[send_rows], "ctx", split_axis=0, concat_axis=0, tiled=True),
        lax.all_to_all(value_tiles[send_rows], "ctx", split_axis=0, concat_axis=0, tiled=True),
    )
    my_owner = lax.dynamic_index_in_dim(owners, ctx_index, 0, keepdims=False)
    my_rank = lax.dynamic_index_in_dim(ranking, ctx_index, 0, keepdims=False)
    slot_ids = my_owner * slot_count + my_rank
    selected_key_rows = fetched_k.reshape(ctx_count * slot_count, BLOCK, head_dim)[
        slot_ids
    ].reshape(block_count, SELECTED * BLOCK, head_dim)
    selected_value_rows = fetched_v.reshape(ctx_count * slot_count, BLOCK, head_dim)[
        slot_ids
    ].reshape(block_count, SELECTED * BLOCK, head_dim)
    inv_root = head_dim ** (-0.5)
    query_block_picks = local_q.reshape(block_count, BLOCK, group_heads, head_dim)
    group_block_picks = local_g.reshape(block_count, BLOCK, group_heads, head_dim)
    scores = (
        jnp.einsum(
            "aeil,acl->aiec",
            query_block_picks,
            selected_key_rows,
            preferred_element_type=jnp.float32,
        )
        * inv_root
    )
    row_peak = jnp.max(scores, axis=-1, keepdims=True)
    lifted = jnp.exp(scores - row_peak)
    attend = lifted / jnp.sum(lifted, axis=-1, keepdims=True)
    grad_weights = jnp.einsum(
        "aeil,acl->aiec", group_block_picks, selected_value_rows, preferred_element_type=jnp.float32
    )
    row_delta = jnp.sum(attend * grad_weights, axis=-1, keepdims=True)
    score_gradient = (attend * (grad_weights - row_delta) * inv_root).astype(jnp.bfloat16)
    half_attention_weights = attend.astype(jnp.bfloat16)
    blank = jnp.zeros((ctx_count * slot_count, BLOCK, head_dim), jnp.float32)

    def place(part_terms):
        return (
            blank.at[slot_ids]
            .set(part_terms.reshape(wanted, BLOCK, head_dim))
            .reshape(ctx_count, slot_count, BLOCK, head_dim)
        )

    query_gradient = jnp.einsum(
        "vpex,vxl->vepl", score_gradient, selected_key_rows, preferred_element_type=jnp.float32
    )
    dkey_part = jnp.einsum(
        "zrny,znrl->zyl", score_gradient, query_block_picks, preferred_element_type=jnp.float32
    )
    dvalue_part = jnp.einsum(
        "zrny,znrl->zyl",
        half_attention_weights,
        group_block_picks,
        preferred_element_type=jnp.float32,
    )
    key_back = send_key_terms(place(dkey_part))
    value_back = send_value_terms(place(dvalue_part))
    query_gradient = query_gradient.astype(jnp.bfloat16).reshape(query_rows, group_heads, head_dim)
    flat_rows = send_rows.reshape(-1)
    flat_fill = filled.reshape(-1)
    key_flat = key_back.reshape(ctx_count * slot_count, BLOCK * head_dim)
    value_flat = value_back.reshape(ctx_count * slot_count, BLOCK * head_dim)
    weight_fill = flat_fill.astype(jnp.float32)[:, None]
    key_sum = jax.ops.segment_sum(key_flat * weight_fill, flat_rows, num_segments=owned)
    value_sum = jax.ops.segment_sum(value_flat * weight_fill, flat_rows, num_segments=owned)
    query_grad = lax.all_to_all(query_gradient, "head", split_axis=0, concat_axis=1, tiled=True)
    key_grad = key_sum.reshape(keys.shape).astype(jnp.bfloat16)
    value_grad = value_sum.reshape(values.shape).astype(jnp.bfloat16)
    return (query_grad, key_grad, value_grad)


def solution(mesh):
    placed = (
        P(("ctx", "head"), None, None),
        P("ctx", "head", None),
        P("ctx", "head", None),
        P(("ctx", "head"), None, None),
        P("head", None, None),
    )
    return jax.shard_map(
        per_device,
        mesh=mesh,
        in_specs=placed,
        out_specs=(P(("ctx", "head"), None, None), P("ctx", "head", None), P("ctx", "head", None)),
        check_vma=False,
    )
```

profile of v0, /device:TPU:6, one launch (start us, length us, event | category | flops | bytes accessed | tf_op | source)
XLA Modules:
  0.0 296.9 jit_solution(5999305387775978523)
XLA Ops:
  0.6 1.8 copy.87
  2.5 16.8 %all-to-all-start.3 = ((bf16[12,64,128]{2,0,1:T(8,128)(2,1)}), bf16[12,64,128]{2,0,1:T(8,128)(2,1)S(1)}, u32[]{:S(2)}, u32[]{:S(2)}) async-start(bf16[12,64,128]{2,0,1:T(8,128)(2,1)} %copy.87), calls=%async_computation.3 | async-start | bytes 524288 | tf_op jit(solution)/shard_map/all_to_all | solution.py:23
  19.3 0.9 copy.74
  20.4 0.5 convert_reduce_fusion
  21.0 0.1 eq.49
  21.1 1.8 copy.84
  22.9 0.2 fusion.54
  23.0 7.4 %all-to-all-done.3 = bf16[12,64,128]{2,0,1:T(8,128)(2,1)S(1)} async-done(((bf16[12,64,128]{2,0,1:T(8,128)(2,1)}), bf16[12,64,128]{2,0,1:T(8,128)(2,1)S(1)}, u32[]{:S(2)}, u32[]{:S(2)}) %all-to-all-start.3) | async-done | bytes 196640 | tf_op jit(solution)/shard_map/all_to_all | solution.py:23
  30.4 3.5 %all-to-all-start.1 = ((bf16[12,64,128]{2,0,1:T(8,128)(2,1)}), bf16[12,64,128]{2,0,1:T(8,128)(2,1)S(1)}, u32[]{:S(2)}, u32[]{:S(2)}) async-start(bf16[12,64,128]{2,0,1:T(8,128)(2,1)} %copy.84), calls=%async_computation.1 | async-start | bytes 524288 | tf_op jit(solution)/shard_map/all_to_all | solution.py:22
  34.0 0.1 fusion.41
  34.1 0.1 reduce_sum.49
  34.3 0.1 reduce_sum.50
  34.4 1.7 gather_fusion
  36.1 9.2 %all-to-all-done.1 = bf16[12,64,128]{2,0,1:T(8,128)(2,1)S(1)} async-done(((bf16[12,64,128]{2,0,1:T(8,128)(2,1)}), bf16[12,64,128]{2,0,1:T(8,128)(2,1)S(1)}, u32[]{:S(2)}, u32[]{:S(2)}) %all-to-all-start.1) | async-done | bytes 196640 | tf_op jit(solution)/shard_map/all_to_all | solution.py:22
  45.3 0.7 copy-done.2
  46.0 13.6 %all-to-all-start = ((bf16[64,1,64,128]{3,2,1,0:T(8,128)(2,1)}), bf16[64,1,64,128]{3,2,1,0:T(8,128)(2,1)S(1)}, u32[]{:S(2)}, u32[]{:S(2)}) async-start(bf16[64,1,64,128]{3,2,1,0:T(8,128)(2,1)} %bitcast.3), calls=%async_computation | async-start | bytes 2097152 | tf_op jit(solution)/shard_map/all_to_all | solution.py:43
  59.6 1.7 gather_fusion.2
  61.3 28.8 %all-to-all-done = bf16[64,1,64,128]{3,2,1,0:T(8,128)(2,1)S(1)} async-done(((bf16[64,1,64,128]{3,2,1,0:T(8,128)(2,1)}), bf16[64,1,64,128]{3,2,1,0:T(8,128)(2,1)S(1)}, u32[]{:S(2)}, u32[]{:S(2)}) %all-to-all-start) | async-done | bytes 1048608 | tf_op jit(solution)/shard_map/all_to_all | solution.py:43
  90.1 6.4 %all-to-all-start.2 = ((bf16[64,1,64,128]{3,2,1,0:T(8,128)(2,1)}), bf16[64,1,64,128]{3,2,1,0:T(8,128)(2,1)S(1)}, u32[]{:S(2)}, u32[]{:S(2)}) async-start(bf16[64,1,64,128]{3,2,1,0:T(8,128)(2,1)} %bitcast.16), calls=%async_computation.2 | async-start | bytes 2097152 | tf_op jit(solution)/shard_map/all_to_all | solution.py:44
  96.4 0.2 add_reduce_fusion
  96.7 0.8 copy.88
  97.4 1.7 copy.85
  99.1 1.6 gather_fusion.1
  100.7 25.2 %all-to-all-done.2 = bf16[64,1,64,128]{3,2,1,0:T(8,128)(2,1)S(1)} async-done(((bf16[64,1,64,128]{3,2,1,0:T(8,128)(2,1)}), bf16[64,1,64,128]{3,2,1,0:T(8,128)(2,1)S(1)}, u32[]{:S(2)}, u32[]{:S(2)}) %all-to-all-start.2) | async-done | bytes 1048608 | tf_op jit(solution)/shard_map/all_to_all | solution.py:44
  126.0 0.7 gather_fusion.3
  126.7 3.2 %fusion.29 = f32[3,1024,64,4]{1,2,3,0:T(8,128)} fusion(bf16[3,1024,128,1]{2,1,3,0:T(8,128)(2,1)S(1)} %bitcast.108, bf16[3,64,4,128]{3,2,1,0:T(4,128)(2,1)} %bitcast.114), kind=kOutput, calls=%fused_computation.42 | convolution fusion | flops 201326592 | bytes 4128768 | tf_op jit(solution)/shard_map/aeil,acl->aiec/dot_general | solution.py:70
  129.9 2.7 fusion.56
  132.6 8.5 %fusion.21 = bf16[3,64,4,128]{3,1,2,0:T(8,128)(2,1)S(1)} fusion(bf16[3,1024,128,1]{2,1,3,0:T(8,128)(2,1)S(1)} %bitcast.117, f32[3,1024,64,4]{1,2,3,0:T(8,128)} %fusion.29, f32[3,4,64,1024]{3,2,1,0:T(8,128)} %get-tuple-element.6, f32[3,4,64]{2,1,0:T(4,128)S(1)} %get-tuple-element.5), kind=kOutput, calls=%fused_computation.35 | convolution fusion | flops 206931712 | bytes 7277568 | tf_op jit(solution)/shard_map/vpex,vxl->vepl/dot_general | solution.py:85
  141.1 0.8 copy.91
  142.0 3.5 %all-to-all-start.4 = ((bf16[192,4,128]{2,1,0:T(4,128)(2,1)}), bf16[192,4,128]{2,1,0:T(4,128)(2,1)S(1)}, u32[]{:S(2)}, u32[]{:S(2)}) async-start(bf16[192,4,128]{2,1,0:T(4,128)(2,1)} %copy.91), calls=%async_computation.4 | async-start | bytes 393216 | tf_op jit(solution)/shard_map/all_to_all | solution.py:107
  145.5 9.8 %fusion.18 = f32[3,1024,128,1]{2,1,3,0:T(8,128)S(1)} fusion(f32[3,1024,64,4]{1,2,3,0:T(8,128)} %fusion.29, bf16[3,64,4,128]{3,2,1,0:T(4,128)(2,1)S(1)} %bitcast.121, f32[3,4,64,1024]{3,2,1,0:T(8,128)} %get-tuple-element.6, f32[3,4,64]{2,1,0:T(4,128)S(1)} %get-tuple-element.5), kind=kOutput, calls=%fused_computation.31 | convolution fusion | flops 206833408 | bytes 8064000 | tf_op jit(solution)/shard_map/zrny,znrl->zyl/dot_general | solution.py:88
  155.3 1.6 broadcast_in_dim.3.clone
  156.9 6.6 %scatter_fusion = f32[64,64,128]{2,1,0:T(8,128)} fusion(f32[64,64,128]{2,1,0:T(8,128)} %broadcast_in_dim.3.clone, s32[48]{0:T(128)S(1)} %fusion.48, f32[48,64,128]{2,1,0:T(8,128)S(1)} %bitcast.111), kind=kCustom, calls=%fused_computation.4 | custom fusion | bytes 4718784 | tf_op jit(solution)/shard_map/scatter | solution.py:81
  163.5 6.5 %all-to-all-start.5 = ((f32[64,1,64,128]{3,2,1,0:T(8,128)}), f32[64,1,64,128]{3,2,1,0:T(8,128)S(1)}, u32[]{:S(2)}, u32[]{:S(2)}) async-start(f32[64,1,64,128]{3,2,1,0:T(8,128)} %bitcast.34), calls=%async_computation.5 | async-start | bytes 4194304 | tf_op jit(solution)/shard_map/all_to_all | solution.py:11
  170.0 3.9 %fusion.14 = f32[3,1024,128,1]{2,1,3,0:T(8,128)} fusion(bf16[3,64,4,128]{3,2,1,0:T(4,128)(2,1)S(1)} %bitcast.115, f32[3,4,64,1024]{3,2,1,0:T(8,128)} %get-tuple-element.6, f32[3,4,64]{2,1,0:T(4,128)S(1)} %get-tuple-element.5), kind=kOutput, calls=%fused_computation.26 | convolution fusion | flops 202899456 | bytes 4918272 | tf_op jit(solution)/shard_map/zrny,znrl->zyl/dot_general | solution.py:91
  173.9 1.6 broadcast_in_dim.3.clone.1
  175.4 7.6 %scatter_fusion.1 = f32[64,64,128]{2,1,0:T(8,128)} fusion(f32[64,64,128]{2,1,0:T(8,128)} %broadcast_in_dim.3.clone.1, s32[48]{0:T(128)S(1)} %fusion.48, f32[48,64,128]{2,1,0:T(8,128)} %bitcast.110), kind=kCustom, calls=%fused_computation.6 | custom fusion | bytes 4718784 | tf_op jit(solution)/shard_map/scatter | solution.py:81
  183.0 42.8 %all-to-all-done.5 = f32[64,1,64,128]{3,2,1,0:T(8,128)S(1)} async-done(((f32[64,1,64,128]{3,2,1,0:T(8,128)}), f32[64,1,64,128]{3,2,1,0:T(8,128)S(1)}, u32[]{:S(2)}, u32[]{:S(2)}) %all-to-all-start.5) | async-done | bytes 2097184 | tf_op jit(solution)/shard_map/all_to_all | solution.py:11
  225.9 10.0 %all-to-all-start.6 = ((f32[64,1,64,128]{3,2,1,0:T(8,128)}), f32[64,1,64,128]{3,2,1,0:T(8,128)}, u32[]{:S(2)}, u32[]{:S(2)}) async-start(f32[64,1,64,128]{3,2,1,0:T(8,128)} %bitcast.40), calls=%async_computation.6 | async-start | bytes 4194304 | tf_op jit(solution)/shard_map/all_to_all | solution.py:15
  235.9 0.1 reduce_or.14
  236.0 0.1 reduce_or.18
  236.1 0.8 copy.92
  236.9 5.2 %scatter_custom_fusion.1 = f32[32,8192]{1,0:T(8,128)} fusion(s32[64]{0:T(128)S(1)} %reduce_sum.50, f32[8,8,64,128]{3,2,1,0:T(8,128)S(1)} %bitcast.105, f32[64]{0:T(128)S(1)} %convert_element_type.54, f32[]{:T(128)} %constant.55.clone.1), kind=kCustom, calls=%fused_computation.24 | custom fusion | flops 1048576 | bytes 3146244 | tf_op jit(solution)/shard_map/scatter-add | solution.py:105
  242.1 1.3 convert_element_type.55
  243.4 1.0 convert_element_type.56
  244.4 45.9 %all-to-all-done.6 = f32[64,1,64,128]{3,2,1,0:T(8,128)} async-done(((f32[64,1,64,128]{3,2,1,0:T(8,128)}), f32[64,1,64,128]{3,2,1,0:T(8,128)}, u32[]{:S(2)}, u32[]{:S(2)}) %all-to-all-start.6) | async-done | bytes 2097184 | tf_op jit(solution)/shard_map/all_to_all | solution.py:15
  290.3 5.5 %scatter_custom_fusion.3 = f32[32,8192]{1,0:T(8,128)S(1)} fusion(s32[64]{0:T(128)S(1)} %reduce_sum.50, f32[8,8,64,128]{3,2,1,0:T(8,128)} %bitcast.52, f32[64]{0:T(128)S(1)} %convert_element_type.54, f32[]{:T(128)} %constant.55.clone.1), kind=kCustom, calls=%fused_computation.21 | custom fusion | flops 1048576 | bytes 3146244 | tf_op jit(solution)/shard_map/scatter-add | solution.py:106
  295.9 1.0 convert_element_type.59
  (25 shorter events, 0.4 us)
Async XLA Ops:
  0.6 33.8 %copy-start = (bf16[2048,1,128]{2,0,1:T(8,128)(2,1)S(1)}, bf16[2048,1,128]{2,0,1:T(8,128)(2,1)}, u32[]{:S(2)}) copy-start(bf16[2048,1,128]{2,0,1:T(8,128)(2,1)} %param.6) | copy-start | bytes 1572868
  2.5 28.0 %all-to-all-start.3 = ((bf16[12,64,128]{2,0,1:T(8,128)(2,1)}), bf16[12,64,128]{2,0,1:T(8,128)(2,1)S(1)}, u32[]{:S(2)}, u32[]{:S(2)}) async-start(bf16[12,64,128]{2,0,1:T(8,128)(2,1)} %copy.87), calls=%async_computation.3 | async-start | bytes 524288 | tf_op jit(solution)/shard_map/all_to_all | solution.py:23
  19.3 40.3 %copy-start.1 = (bf16[2048,1,128]{2,0,1:T(8,128)(2,1)S(1)}, bf16[2048,1,128]{2,0,1:T(8,128)(2,1)}, u32[]{:S(2)}) copy-start(bf16[2048,1,128]{2,0,1:T(8,128)(2,1)} %param.7) | copy-start | bytes 1572868
  30.4 14.9 %all-to-all-start.1 = ((bf16[12,64,128]{2,0,1:T(8,128)(2,1)}), bf16[12,64,128]{2,0,1:T(8,128)(2,1)S(1)}, u32[]{:S(2)}, u32[]{:S(2)}) async-start(bf16[12,64,128]{2,0,1:T(8,128)(2,1)} %copy.84), calls=%async_computation.1 | async-start | bytes 524288 | tf_op jit(solution)/shard_map/all_to_all | solution.py:22
  45.3 0.7 copy-start.2
  46.0 44.1 %all-to-all-start = ((bf16[64,1,64,128]{3,2,1,0:T(8,128)(2,1)}), bf16[64,1,64,128]{3,2,1,0:T(8,128)(2,1)S(1)}, u32[]{:S(2)}, u32[]{:S(2)}) async-start(bf16[64,1,64,128]{3,2,1,0:T(8,128)(2,1)} %bitcast.3), calls=%async_computation | async-start | bytes 2097152 | tf_op jit(solution)/shard_map/all_to_all | solution.py:43
  90.1 35.9 %all-to-all-start.2 = ((bf16[64,1,64,128]{3,2,1,0:T(8,128)(2,1)}), bf16[64,1,64,128]{3,2,1,0:T(8,128)(2,1)S(1)}, u32[]{:S(2)}, u32[]{:S(2)}) async-start(bf16[64,1,64,128]{3,2,1,0:T(8,128)(2,1)} %bitcast.16), calls=%async_computation.2 | async-start | bytes 2097152 | tf_op jit(solution)/shard_map/all_to_all | solution.py:44
  100.7 29.2 %copy-start.4 = (bf16[48,64,128]{2,1,0:T(8,128)(2,1)S(1)}, bf16[48,64,128]{2,1,0:T(8,128)(2,1)}, u32[]{:S(2)}) copy-start(bf16[48,64,128]{2,1,0:T(8,128)(2,1)} %gather_fusion.1) | copy-start | bytes 2359300
  100.7 29.2 %copy-start.5 = (bf16[12,16,4,128]{3,2,0,1:T(4,128)(2,1)S(1)}, bf16[12,16,4,128]{3,2,0,1:T(4,128)(2,1)}, u32[]{:S(2)}) copy-start(bf16[12,16,4,128]{3,2,0,1:T(4,128)(2,1)} %copy.85) | copy-start | bytes 589828
  142.0 21.5 %all-to-all-start.4 = ((bf16[192,4,128]{2,1,0:T(4,128)(2,1)}), bf16[192,4,128]{2,1,0:T(4,128)(2,1)S(1)}, u32[]{:S(2)}, u32[]{:S(2)}) async-start(bf16[192,4,128]{2,1,0:T(4,128)(2,1)} %copy.91), calls=%async_computation.4 | async-start | bytes 393216 | tf_op jit(solution)/shard_map/all_to_all | solution.py:107
  163.5 6.5 %copy-start.3 = (bf16[12,16,4,128]{3,2,0,1:T(4,128)(2,1)S(1)}, bf16[12,16,4,128]{3,2,0,1:T(4,128)(2,1)}, u32[]{:S(2)}) copy-start(bf16[12,16,4,128]{3,2,0,1:T(4,128)(2,1)} %copy.88) | copy-start | bytes 589828
  163.5 62.4 %all-to-all-start.5 = ((f32[64,1,64,128]{3,2,1,0:T(8,128)}), f32[64,1,64,128]{3,2,1,0:T(8,128)S(1)}, u32[]{:S(2)}, u32[]{:S(2)}) async-start(f32[64,1,64,128]{3,2,1,0:T(8,128)} %bitcast.34), calls=%async_computation.5 | async-start | bytes 4194304 | tf_op jit(solution)/shard_map/all_to_all | solution.py:11
  225.9 64.4 %all-to-all-start.6 = ((f32[64,1,64,128]{3,2,1,0:T(8,128)}), f32[64,1,64,128]{3,2,1,0:T(8,128)}, u32[]{:S(2)}, u32[]{:S(2)}) async-start(f32[64,1,64,128]{3,2,1,0:T(8,128)} %bitcast.40), calls=%async_computation.6 | async-start | bytes 4194304 | tf_op jit(solution)/shard_map/all_to_all | solution.py:15
where the time goes:
time: 298 us; the launch traced here: 297 us
  waiting for transfers between devices  159 us (53%)
  starting transfers between devices  60.2 us (20%)
  local copies, waits for them, and re-layouts  35 us (12%)
  matrix products  28.1 us (9%)
  other arithmetic  13.3 us (4%)
    all_to_all x1, waiting for transfers between devices, send_value_terms(): lax.all_to_all(placed, 'ctx', split_axis=0, concat_axis=0, tiled=True)  45.9 us
    all_to_all x1, waiting for transfers between devices, send_key_terms(): lax.all_to_all(placed, 'ctx', split_axis=0, concat_axis=0, tiled=True)  42.8 us
    all_to_all x1, waiting for transfers between devices, per_device(): lax.all_to_all(key_tiles[send_rows], 'ctx', split_axis=0, concat_axis=0,...  28.8 us
    all_to_all x1, waiting for transfers between devices, per_device(): lax.all_to_all(value_tiles[send_rows], 'ctx', split_axis=0, concat_axis=0...  25.2 us
    all_to_all x1, starting transfers between devices, per_device(): lax.all_to_all(out_grad, 'head', split_axis=1, concat_axis=0, tiled=True)  16.8 us
    scatter x2, local copies, waits for them, and re-layouts, place(): return blank.at[slot_ids].set(part_terms.reshape(wanted, BLOCK, head_dim)...  14.2 us
    all_to_all x1, starting transfers between devices, per_device(): lax.all_to_all(key_tiles[send_rows], 'ctx', split_axis=0, concat_axis=0,...  13.6 us
    all_to_all x1, starting transfers between devices, send_value_terms(): lax.all_to_all(placed, 'ctx', split_axis=0, concat_axis=0, tiled=True)  9.99 us
  transfers between devices with their start and end apart: 7, of which 6 were waited for; matrix products, arithmetic and copies ran while one was open for 17% of the time, Pallas kernels for 0%

commit v1 on v0

v1 whole, which is shorter than its diff:
```python
import functools

import jax
import jax.numpy as jnp
from jax import lax
from jax.experimental import pallas as pl
from jax.experimental.pallas import tpu as pltpu
from jax.sharding import PartitionSpec as P

BLOCK = 64
SELECTED = 16
CTX = 64
OWNED = 32
QBLOCKS = 3
HEAD_DIM = 128
GROUP_HEADS = 4
ROWS = BLOCK * GROUP_HEADS
PART = 16
SCALE = HEAD_DIM**-0.5
LOG2E = 1.4426950408889634
VMEM_LIMIT = 40 * 1024 * 1024


def wanted_row(rows, index):
    first = rows[QBLOCKS * index]
    return jnp.maximum(jnp.maximum(first, rows[QBLOCKS * index + 1]), rows[QBLOCKS * index + 2])


def pack_kernel(rows, keys, values, packed):
    base = pl.program_id(0) * PART

    def copy(index, carry):
        row = jnp.maximum(wanted_row(rows, base + index), 0)
        packed[index, 0] = keys[row]
        packed[index, 1] = values[row]
        return carry

    lax.fori_loop(0, PART, copy, 0, unroll=4)


def pack(rows, keys, values):
    whole = pl.BlockSpec((OWNED, BLOCK, HEAD_DIM), lambda i, rows: (0, 0, 0))
    return pl.pallas_call(
        pack_kernel,
        out_shape=jax.ShapeDtypeStruct((CTX, 2, BLOCK, HEAD_DIM), jnp.bfloat16),
        grid_spec=pltpu.PrefetchScalarGridSpec(
            num_scalar_prefetch=1,
            grid=(CTX // PART,),
            in_specs=[whole, whole],
            out_specs=pl.BlockSpec((PART, 2, BLOCK, HEAD_DIM), lambda i, rows: (i, 0, 0, 0)),
        ),
        compiler_params=pltpu.CompilerParams(vmem_limit_bytes=VMEM_LIMIT),
        name="pack_blocks",
    )(rows, keys, values)


def attend_kernel(slots, fetched, queries, grads, query_grad, terms, key_rows, value_rows):
    step = pl.program_id(0)

    @pl.when(step == 0)
    def _():
        terms[...] = jnp.zeros_like(terms)

    for s in range(SELECTED):
        slot = slots[s, step]
        key_rows[pl.ds(s * BLOCK, BLOCK), :] = fetched[slot, 0]
        value_rows[pl.ds(s * BLOCK, BLOCK), :] = fetched[slot, 1]
    q_now = queries[...]
    g_now = grads[...]
    rows_last = (((1,), (1,)), ((), ()))
    rows_first = (((0,), (0,)), ((), ()))
    scores = lax.dot_general(key_rows[...], q_now, rows_last, preferred_element_type=jnp.float32)
    peak = jnp.max(scores, axis=0, keepdims=True)
    lifted = jnp.exp2((scores - peak) * (SCALE * LOG2E))
    inverse = 1.0 / jnp.sum(lifted, axis=0, keepdims=True)
    attend = lifted * inverse
    weights = lax.dot_general(value_rows[...], g_now, rows_last, preferred_element_type=jnp.float32)
    delta = jnp.sum(attend * weights, axis=0, keepdims=True)
    score_grad = (attend * (weights - delta) * SCALE).astype(jnp.bfloat16)
    half = attend.astype(jnp.bfloat16)
    flipped = lax.dot_general(key_rows[...], score_grad, rows_first, preferred_element_type=jnp.float32)
    query_grad[...] = flipped.T.astype(jnp.bfloat16)
    key_terms = jnp.dot(score_grad, q_now, preferred_element_type=jnp.float32).astype(jnp.bfloat16)
    value_terms = jnp.dot(half, g_now, preferred_element_type=jnp.float32).astype(jnp.bfloat16)
    for s in range(SELECTED):
        slot = slots[s, step]
        terms[slot, 0] = key_terms[s * BLOCK : (s + 1) * BLOCK]
        terms[slot, 1] = value_terms[s * BLOCK : (s + 1) * BLOCK]


def attend_backward(slots, fetched, queries, grads):
    whole = pl.BlockSpec((CTX, 2, BLOCK, HEAD_DIM), lambda i, slots: (0, 0, 0, 0))
    part = pl.BlockSpec((ROWS, HEAD_DIM), lambda i, slots: (i, 0))
    return pl.pallas_call(
        attend_kernel,
        out_shape=(
            jax.ShapeDtypeStruct((QBLOCKS * ROWS, HEAD_DIM), jnp.bfloat16),
            jax.ShapeDtypeStruct((CTX, 2, BLOCK, HEAD_DIM), jnp.bfloat16),
        ),
        grid_spec=pltpu.PrefetchScalarGridSpec(
            num_scalar_prefetch=1,
            grid=(QBLOCKS,),
            in_specs=[whole, part, part],
            out_specs=(part, whole),
            scratch_shapes=[
                pltpu.VMEM((SELECTED * BLOCK, HEAD_DIM), jnp.bfloat16),
                pltpu.VMEM((SELECTED * BLOCK, HEAD_DIM), jnp.bfloat16),
            ],
        ),
        compiler_params=pltpu.CompilerParams(vmem_limit_bytes=VMEM_LIMIT),
        name="attend_backward",
    )(slots, fetched, queries, grads)


def sum_kernel(rows, terms, key_grad, value_grad, key_sum, value_sum):
    step = pl.program_id(0)

    @pl.when(step == 0)
    def _():
        key_sum[...] = jnp.zeros_like(key_sum)
        value_sum[...] = jnp.zeros_like(value_sum)

    def add(index, carry):
        row = wanted_row(rows, step * PART + index)

        @pl.when(row >= 0)
        def _():
            key_sum[row] += terms[index, 0].astype(jnp.float32)
            value_sum[row] += terms[index, 1].astype(jnp.float32)

        return carry

    lax.fori_loop(0, PART, add, 0)

    @pl.when(step == pl.num_programs(0) - 1)
    def _():
        key_grad[...] = key_sum[...].astype(jnp.bfloat16)
        value_grad[...] = value_sum[...].astype(jnp.bfloat16)


def owner_sum(rows, terms):
    whole = pl.BlockSpec((OWNED, BLOCK, HEAD_DIM), lambda i, rows: (0, 0, 0))
    grad = jax.ShapeDtypeStruct((OWNED, BLOCK, HEAD_DIM), jnp.bfloat16)
    return pl.pallas_call(
        sum_kernel,
        out_shape=(grad, grad),
        grid_spec=pltpu.PrefetchScalarGridSpec(
            num_scalar_prefetch=1,
            grid=(CTX // PART,),
            in_specs=[pl.BlockSpec((PART, 2, BLOCK, HEAD_DIM), lambda i, rows: (i, 0, 0, 0))],
            out_specs=(whole, whole),
            scratch_shapes=[
                pltpu.VMEM((OWNED, BLOCK, HEAD_DIM), jnp.float32),
                pltpu.VMEM((OWNED, BLOCK, HEAD_DIM), jnp.float32),
            ],
        ),
        compiler_params=pltpu.CompilerParams(vmem_limit_bytes=VMEM_LIMIT),
        name="owner_sum",
    )(rows, terms)


def exchange(blocks):
    return lax.all_to_all(blocks, "ctx", split_axis=0, concat_axis=0, tiled=True)


def my_heads(tokens, head):
    gathered = lax.all_gather(tokens, "head", axis=0, tiled=True)
    mine = lax.dynamic_slice_in_dim(gathered, head * GROUP_HEADS, GROUP_HEADS, 1)
    return mine.reshape(QBLOCKS * ROWS, HEAD_DIM)


def per_device(queries, keys, values, out_grad, selected):
    ctx, head = lax.axis_index("ctx"), lax.axis_index("head")
    table = selected[0].T
    rows = jnp.max(jnp.where(table // OWNED == ctx, table % OWNED, -1), axis=0)
    slots = lax.dynamic_slice_in_dim(table, ctx * QBLOCKS, QBLOCKS, 1) // OWNED
    blocks = (OWNED, BLOCK, HEAD_DIM)
    packed = pack(rows, keys.reshape(blocks), values.reshape(blocks))
    fetched = exchange(packed)
    query_grad, terms = attend_backward(slots, fetched, my_heads(queries, head), my_heads(out_grad, head))
    back = exchange(terms)
    tokens = queries.shape[0]
    gathered = lax.all_gather(query_grad, "head", axis=0)
    mine = lax.dynamic_slice_in_dim(gathered, head * tokens * GROUP_HEADS, tokens * GROUP_HEADS, 1)
    mine = mine.reshape(gathered.shape[0], tokens, GROUP_HEADS, HEAD_DIM)
    query_grad = mine.transpose(1, 0, 2, 3).reshape(queries.shape)
    key_grad, value_grad = owner_sum(rows, back)
    return query_grad, key_grad.reshape(keys.shape), value_grad.reshape(values.shape)


def solution(mesh):
    tokens = P(("ctx", "head"), None, None)
    context = P("ctx", "head", None)
    return jax.shard_map(
        per_device,
        mesh=mesh,
        in_specs=(tokens, context, context, tokens, P("head", None, None)),
        out_specs=(tokens, context, context),
        check_vma=False,
    )
```

time: 298 us -> 207 us (0.69)
  the two profiles are of different devices: /device:TPU:6 before, /device:TPU:126 now
where the time goes in v1:
time: 207 us
  waiting for transfers between devices  144 us (70%)
  starting transfers between devices  28.8 us (14%)
  between operations  13.8 us (7%)
  Pallas kernels  10.2 us (5%)
  local copies, waits for them, and re-layouts  8.73 us (4%)
    all_gather x2, waiting for transfers between devices, my_heads(): gathered = lax.all_gather(tokens, 'head', axis=0, tiled=True)  86.7 us
    all_to_all x2, waiting for transfers between devices, exchange(): lax.all_to_all(blocks, 'ctx', split_axis=0, concat_axis=0, tiled=True)  56.2 us
    all_to_all x2, starting transfers between devices, exchange(): lax.all_to_all(blocks, 'ctx', split_axis=0, concat_axis=0, tiled=True)  28.7 us
    pallas_call x1, Pallas kernels, attend_backward(): pl.pallas_call(attend_kernel, out_shape=(jax.ShapeDtypeStruct((QBLOCKS *...  5.87 us
    unnamed x11, local copies, waits for them, and re-layouts  4.83 us
  transfers between devices with their start and end apart: 5, of which 3 were waited for; matrix products, arithmetic and copies ran while one was open for 1% of the time, Pallas kernels for 2%

profile of v1, /device:TPU:126, one launch (start us, length us, event | category | flops | bytes accessed | tf_op | source)
XLA Modules:
  0.0 206.8 jit_solution(5946278260299066228)
XLA Ops:
  7.2 0.0 all-gather.5.cloned.1.call-start
  7.2 0.7 all-gather.5.cloned.1.call-update
  7.9 0.0 all-gather.7.cloned.1.call-start
  7.9 0.7 all-gather.7.cloned.1.call-update
  8.7 0.8 fusion.2.rows
  9.4 0.0 copy-start.2
  9.4 1.0 copy-done.2
  10.4 0.0 copy-start.3
  10.5 1.0 copy-done.3
  11.5 0.0 copy-start.4
  11.5 1.0 pack_blocks.1
  12.5 0.0 copy-start
  12.5 1.3 copy-done
  13.9 16.0 %all-to-all-start = ((bf16[64,2,64,128]{3,2,1,0:T(8,128)(2,1)}), bf16[64,2,64,128]{3,2,1,0:T(8,128)(2,1)S(1)}, u32[]{:S(2)}, u32[]{:S(2)}) async-start(bf16[64,2,64,128]{3,2,1,0:T(8,128)(2,1)} %copy-done), calls=%async_computation | async-start | bytes 4194304 | tf_op jit(solution)/shard_map/all_to_all | solution.py:163
  29.8 0.0 all-gather.9.cloned.1.call-start
  29.9 0.0 copy-done.4
  29.9 0.1 add_select_fusion.2.slots
  30.0 39.1 %all-gather.5.cloned.1.call-done = bf16[192,64,128]{2,1,0:T(8,128)(2,1)} async-done(((bf16[12,64,128]{2,1,0:T(8,128)(2,1)}), bf16[192,64,128]{2,1,0:T(8,128)(2,1)}) %all-gather.5.cloned.1.call-update) | async-done | bytes 3145744 | tf_op jit(solution)/shard_map/all_gather | solution.py:167
  69.1 1.1 constant_dynamic-slice_fusion.1
  70.2 47.6 %all-gather.7.cloned.1.call-done = bf16[192,64,128]{2,1,0:T(8,128)(2,1)} async-done(((bf16[12,64,128]{2,1,0:T(8,128)(2,1)}), bf16[192,64,128]{2,1,0:T(8,128)(2,1)}) %all-gather.7.cloned.1.call-update) | async-done | bytes 3145744 | tf_op jit(solution)/shard_map/all_gather | solution.py:167
  117.8 1.1 constant_dynamic-slice_fusion
  118.9 0.0 all-to-all-done.fetched
  118.9 5.9 %attend_backward.1 = (bf16[768,128]{1,0:T(8,128)(2,1)}, bf16[64,2,64,128]{3,2,1,0:T(8,128)(2,1)S(1)}) custom-call(s32[16,3]{1,0:T(8,128)S(1)} %add_select_fusion.2.slots, bf16[64,2,64,128]{3,2,1,0:T(8,128)(2,1)S(1)} %all-to-all-done.fetched, bf16[768,128]{1,0:T(8,128)(2,1)S(1)} %bitcast.49, bf16[768,128]{1,0:T(8,128)(2,1)S(1)} %bitcast.50), custom_call_target="tpu_custom_call" | custom-call | tf_op jit(solution)/shard_map/attend_backward/pallas_call | solution.py:94
  124.8 0.0 copy-start.1
  124.8 1.4 copy-done.1
  126.1 0.0 all-gather.9.cloned.1.call-update
  126.2 12.7 %all-to-all-start.1 = ((bf16[64,2,64,128]{3,2,1,0:T(8,128)(2,1)}), bf16[64,2,64,128]{3,2,1,0:T(8,128)(2,1)S(1)}, u32[]{:S(2)}, u32[]{:S(2)}) async-start(bf16[64,2,64,128]{3,2,1,0:T(8,128)(2,1)} %copy-done.1), calls=%async_computation.1 | async-start | bytes 4194304 | tf_op jit(solution)/shard_map/all_to_all | solution.py:163
  138.9 56.2 %all-to-all-done.1.terms = bf16[64,2,64,128]{3,2,1,0:T(8,128)(2,1)S(1)} async-done(((bf16[64,2,64,128]{3,2,1,0:T(8,128)(2,1)}), bf16[64,2,64,128]{3,2,1,0:T(8,128)(2,1)S(1)}, u32[]{:S(2)}, u32[]{:S(2)}) %all-to-all-start.1) | async-done | bytes 2097184 | tf_op jit(solution)/shard_map/all_to_all | solution.py:163
  195.1 3.3 %owner_sum.1 = (bf16[32,64,128]{2,1,0:T(8,128)(2,1)}, bf16[32,64,128]{2,1,0:T(8,128)(2,1)}) custom-call(s32[192]{0:T(256)S(1)} %fusion.2.rows, bf16[64,2,64,128]{3,2,1,0:T(8,128)(2,1)S(1)} %all-to-all-done.1.terms), custom_call_target="tpu_custom_call" | custom-call | tf_op jit(solution)/shard_map/owner_sum/pallas_call | solution.py:144
  198.5 0.0 all-gather.9.cloned.1.call-done
  198.5 0.9 constant_dynamic-slice_fusion.2
  199.4 0.1 copy.22
  199.5 0.8 copy.20
Async XLA Ops:
  7.2 61.9 %all-gather.5.cloned.1.call-start = ((), (), s32[]{:S(2)}) async-start(), calls=%async_computation.2 | async-start | bytes 3342336 | tf_op jit(solution)/shard_map/all_gather | solution.py:167
  7.9 109.9 %all-gather.7.cloned.1.call-start = ((), (), s32[]{:S(2)}) async-start(), calls=%async_computation.3 | async-start | bytes 3342336 | tf_op jit(solution)/shard_map/all_gather | solution.py:167
  9.4 1.0 copy-start.2
  10.4 1.0 copy-start.3
  11.5 18.4 %copy-start.4 = (s32[1,192,16]{1,2,0:T(8,128)S(1)}, s32[1,192,16]{1,2,0:T(8,128)}, u32[]{:S(2)}) copy-start(s32[1,192,16]{1,2,0:T(8,128)} %param.9) | copy-start | bytes 36868
  12.5 1.4 copy-start
  13.9 105.0 %all-to-all-start = ((bf16[64,2,64,128]{3,2,1,0:T(8,128)(2,1)}), bf16[64,2,64,128]{3,2,1,0:T(8,128)(2,1)S(1)}, u32[]{:S(2)}, u32[]{:S(2)}) async-start(bf16[64,2,64,128]{3,2,1,0:T(8,128)(2,1)} %copy-done), calls=%async_computation | async-start | bytes 4194304 | tf_op jit(solution)/shard_map/all_to_all | solution.py:163
  29.8 168.7 %all-gather.9.cloned.1.call-start = ((), (), s32[]{:S(2)}) async-start(), calls=%async_computation.4 | async-start | bytes 3342336 | tf_op jit(solution)/shard_map/all_gather | solution.py:183
  124.8 1.4 copy-start.1
  126.2 69.0 %all-to-all-start.1 = ((bf16[64,2,64,128]{3,2,1,0:T(8,128)(2,1)}), bf16[64,2,64,128]{3,2,1,0:T(8,128)(2,1)S(1)}, u32[]{:S(2)}, u32[]{:S(2)}) async-start(bf16[64,2,64,128]{3,2,1,0:T(8,128)(2,1)} %copy-done.1), calls=%async_computation.1 | async-start | bytes 4194304 | tf_op jit(solution)/shard_map/all_to_all | solution.py:163
Sparse Core Ops, SparseCore 0:
  10.7 58.3 all-gather.4
  71.8 45.9 all-gather.6
  126.3 45.9 all-gather.8

commit v2 on v1

v2 whole, which is shorter than its diff:
```python
import functools

import jax
import jax.numpy as jnp
from jax import lax
from jax.experimental import pallas as pl
from jax.experimental.pallas import tpu as pltpu
from jax.sharding import PartitionSpec as P

BLOCK = 64
SELECTED = 16
CTX = 64
OWNED = 32
QBLOCKS = 3
QBLOCKS_ALL = 192
HEAD_DIM = 128
GROUP_HEADS = 4
ROWS = BLOCK * GROUP_HEADS
KEYS = SELECTED * BLOCK
TOKENS = 12
PIECE = TOKENS * GROUP_HEADS
PLANES = 8
CORES = 2
SCALE = HEAD_DIM**-0.5
LOG2E = 1.4426950408889634
VMEM_LIMIT = 40 * 1024 * 1024
VMEM_ALL = 62 * 1024 * 1024
VMEM_ATTEND = 52 * 1024 * 1024
BF16 = jnp.bfloat16
F32 = jnp.float32
IN_VMEM = pl.BlockSpec(memory_space=pltpu.VMEM)
IN_SMEM = pl.BlockSpec(memory_space=pltpu.SMEM)
IN_HBM = pl.BlockSpec(memory_space=pltpu.HBM)


def array(*shape, dtype=BF16):
    return jax.ShapeDtypeStruct(shape, dtype)


def wanted_row(rows, index):
    first = rows[0, QBLOCKS * index]
    return jnp.maximum(jnp.maximum(first, rows[0, QBLOCKS * index + 1]), rows[0, QBLOCKS * index + 2])


def pack_kernel(place, table, keys, values, packed, rows, key_buf, value_buf, out_buf, row_buf, in_sems, out_sems):
    loads = [
        pltpu.make_async_copy(keys, key_buf, in_sems.at[0]),
        pltpu.make_async_copy(values, value_buf, in_sems.at[1]),
    ]
    for load in loads:
        load.start()
    picks = table[...]
    mine = jnp.where(picks // OWNED == place[0], picks % OWNED, -1)
    row_buf[...] = jnp.max(mine, axis=0, keepdims=True)
    to_scalars = pltpu.make_async_copy(row_buf, rows, in_sems.at[2])
    to_scalars.start()
    to_scalars.wait()
    for load in loads:
        load.wait()
    parts = out_sems.shape[0]
    size = CTX // parts

    def store(part):
        span = pl.ds(part * size, size)
        return pltpu.make_async_copy(out_buf.at[span], packed.at[span], out_sems.at[part])

    for part in range(parts):

        def copy(index, carry):
            row = jnp.maximum(wanted_row(rows, index), 0)
            out_buf[index, 0] = key_buf[row]
            out_buf[index, 1] = value_buf[row]
            return carry

        lax.fori_loop(part * size, (part + 1) * size, copy, 0, unroll=4)
        store(part).start()
    for part in range(parts):
        store(part).wait()


def pack(place, table, keys, values):
    return pl.pallas_call(
        pack_kernel,
        out_shape=(array(CTX, 2, BLOCK, HEAD_DIM), array(1, QBLOCKS_ALL, dtype=jnp.int32)),
        in_specs=[IN_SMEM, IN_VMEM, IN_HBM, IN_HBM],
        out_specs=(IN_HBM, IN_SMEM),
        scratch_shapes=[
            pltpu.VMEM((OWNED, BLOCK, HEAD_DIM), BF16),
            pltpu.VMEM((OWNED, BLOCK, HEAD_DIM), BF16),
            pltpu.VMEM((CTX, 2, BLOCK, HEAD_DIM), BF16),
            pltpu.VMEM((1, QBLOCKS_ALL), jnp.int32),
            pltpu.SemaphoreType.DMA((3,)),
            pltpu.SemaphoreType.DMA((4,)),
        ],
        compiler_params=pltpu.CompilerParams(vmem_limit_bytes=VMEM_ALL),
        name="pack_blocks",
    )(place, table, keys, values)


def halves(first, second):
    low = lax.broadcasted_iota(jnp.int32, first.shape, first.ndim - 2) < GROUP_HEADS
    axis = first.ndim - 2
    return (
        jnp.where(low, first, pltpu.roll(second, GROUP_HEADS, axis)),
        jnp.where(low, pltpu.roll(first, GROUP_HEADS, axis), second),
    )


def split_kernel(place, rows, queries, grads, keep, send):
    plane, core = place[1], place[2]
    for kind, ref in enumerate((queries, grads)):
        tokens = ref[...].astype(F32).reshape(TOKENS // 2, 2, PLANES, 8, HEAD_DIM)
        low, high = halves(tokens[:, 0], tokens[:, 1])
        mine = jnp.where(core == 0, low, high).astype(BF16)
        other = jnp.where(core == 0, high, low).astype(BF16)
        for target in range(PLANES):
            shift = (target - plane + PLANES) % PLANES
            keep[shift, kind] = mine[:, target].reshape(PIECE, HEAD_DIM)
            send[shift, kind] = other[:, target].reshape(PIECE, HEAD_DIM)


def split(place, rows, queries, grads):
    out = array(PLANES, 2, PIECE, HEAD_DIM)
    return pl.pallas_call(
        split_kernel,
        out_shape=(out, out),
        in_specs=[IN_SMEM, IN_SMEM, IN_VMEM, IN_VMEM],
        out_specs=(IN_VMEM, IN_VMEM),
        compiler_params=pltpu.CompilerParams(vmem_limit_bytes=VMEM_LIMIT),
        name="split_heads",
    )(place, rows, queries, grads)


def join_kernel(keep, got, *parcels):
    for shift, parcel in enumerate(parcels):
        parcel[0:2] = keep[shift]
        parcel[2:4] = got[shift]


def join(keep, got):
    return pl.pallas_call(
        join_kernel,
        out_shape=(array(4, PIECE, HEAD_DIM),) * PLANES,
        in_specs=[IN_VMEM, IN_VMEM],
        out_specs=(IN_VMEM,) * PLANES,
        compiler_params=pltpu.CompilerParams(vmem_limit_bytes=VMEM_LIMIT),
        name="join_parcels",
    )(keep, got)


def attend_kernel(place, slots, fetched, *refs):
    parcels, terms, results = refs[:PLANES], refs[PLANES], refs[PLANES + 1 : 2 * PLANES + 1]
    q_rows, g_rows, key_rows, value_rows, grad_rows, stage, sems, key_sems, value_sems = refs[2 * PLANES + 1 :]
    plane, core = place[1], place[2]

    def load(step, carry):
        for s in range(SELECTED):
            slot = slots[s, step]
            span = pl.ds(pl.multiple_of(step * KEYS + s * BLOCK, BLOCK), BLOCK)
            pltpu.make_async_copy(fetched.at[slot, 0], key_rows.at[span], key_sems.at[step]).start()
            pltpu.make_async_copy(fetched.at[slot, 1], value_rows.at[span], value_sems.at[step]).start()
        return carry

    lax.fori_loop(0, QBLOCKS, load, 0)
    for shift, parcel in enumerate(parcels):
        source = (plane - shift + PLANES) % PLANES
        for piece, owner in ((0, core), (2, 1 - core)):
            span = pl.ds(pl.multiple_of((source * CORES + owner) * PIECE, 16), PIECE)
            q_rows[span, :] = parcel[piece]
            g_rows[span, :] = parcel[piece + 1]
    rows_last = (((1,), (1,)), ((), ()))
    rows_first = (((0,), (0,)), ((), ()))

    def store(step, s):
        item = step * SELECTED + s
        return pltpu.make_async_copy(stage.at[item], terms.at[slots[s, step]], sems.at[item])

    def block(step, carry):
        chosen = pl.ds(pl.multiple_of(step * KEYS, KEYS), KEYS)
        for rows, load_sems in ((key_rows, key_sems), (value_rows, value_sems)):
            pltpu.make_async_copy(rows.at[chosen], rows.at[chosen], load_sems.at[step]).wait()
        k_now, v_now = key_rows[chosen, :], value_rows[chosen, :]
        span = pl.ds(pl.multiple_of(step * ROWS, ROWS), ROWS)
        q_now = q_rows[span, :]
        g_now = g_rows[span, :]
        scores = lax.dot_general(k_now, q_now, rows_last, preferred_element_type=F32)
        peak = jnp.max(scores, axis=0, keepdims=True)
        lifted = jnp.exp2((scores - peak) * (SCALE * LOG2E))
        inverse = 1.0 / jnp.sum(lifted, axis=0, keepdims=True)
        attend = lifted * inverse
        weights = lax.dot_general(v_now, g_now, rows_last, preferred_element_type=F32)
        delta = jnp.sum(attend * weights, axis=0, keepdims=True)
        score_grad = (attend * (weights - delta) * SCALE).astype(BF16)
        half = attend.astype(BF16)
        flipped = lax.dot_general(k_now, score_grad, rows_first, preferred_element_type=F32)
        grad_rows[span, :] = flipped.T.astype(BF16)
        key_terms = jnp.dot(score_grad, q_now, preferred_element_type=F32).astype(BF16)
        value_terms = jnp.dot(half, g_now, preferred_element_type=F32).astype(BF16)
        for s in range(SELECTED):
            item = step * SELECTED + s
            stage[item, 0] = key_terms[s * BLOCK : (s + 1) * BLOCK]
            stage[item, 1] = value_terms[s * BLOCK : (s + 1) * BLOCK]
            store(step, s).start()
        return carry

    lax.fori_loop(0, QBLOCKS, block, 0)
    for shift, result in enumerate(results):
        target = (plane + shift) % PLANES
        for owner in range(CORES):
            span = pl.ds(pl.multiple_of((target * CORES + owner) * PIECE, 16), PIECE)
            result[owner] = grad_rows[span, :]

    def finish(step, carry):
        for s in range(SELECTED):
            store(step, s).wait()
        return carry

    lax.fori_loop(0, QBLOCKS, finish, 0)


def attend_backward(place, slots, fetched, parcels):
    rows = pltpu.VMEM((QBLOCKS * ROWS, HEAD_DIM), BF16)
    return pl.pallas_call(
        attend_kernel,
        out_shape=(array(CTX, 2, BLOCK, HEAD_DIM),) + (array(CORES, PIECE, HEAD_DIM),) * PLANES,
        in_specs=[IN_SMEM, IN_SMEM, IN_HBM] + [IN_VMEM] * PLANES,
        out_specs=(IN_HBM,) + (IN_VMEM,) * PLANES,
        scratch_shapes=[
            rows,
            rows,
            pltpu.VMEM((QBLOCKS * KEYS, HEAD_DIM), BF16),
            pltpu.VMEM((QBLOCKS * KEYS, HEAD_DIM), BF16),
            rows,
            pltpu.VMEM((QBLOCKS * SELECTED, 2, BLOCK, HEAD_DIM), BF16),
            pltpu.SemaphoreType.DMA((QBLOCKS * SELECTED,)),
            pltpu.SemaphoreType.DMA((QBLOCKS,)),
            pltpu.SemaphoreType.DMA((QBLOCKS,)),
        ],
        compiler_params=pltpu.CompilerParams(vmem_limit_bytes=VMEM_ATTEND),
        name="attend_backward",
    )(place, slots, fetched, *parcels)


def swap_kernel(place, *refs):
    parcels, (keep, send) = refs[:PLANES], refs[PLANES:]
    core = place[2]
    for shift, parcel in enumerate(parcels):
        keep[shift] = parcel[core]
        send[shift] = parcel[1 - core]


def swap(place, parcels):
    out = array(PLANES, PIECE, HEAD_DIM)
    return pl.pallas_call(
        swap_kernel,
        out_shape=(out, out),
        in_specs=[IN_SMEM] + [IN_VMEM] * PLANES,
        out_specs=(IN_VMEM, IN_VMEM),
        compiler_params=pltpu.CompilerParams(vmem_limit_bytes=VMEM_LIMIT),
        name="swap_cores",
    )(place, *parcels)


def merge_kernel(place, keep, got, query_grad):
    plane, core = place[1], place[2]
    shape = (TOKENS // 2, 8, HEAD_DIM)
    even, odd = [], []
    for source in range(PLANES):
        shift = (plane - source + PLANES) % PLANES
        mine = keep[shift].astype(F32).reshape(shape)
        other = got[shift].astype(F32).reshape(shape)
        pair = halves(jnp.where(core == 0, mine, other), jnp.where(core == 0, other, mine))
        even.append(pair[0])
        odd.append(pair[1])
    both = jnp.stack([jnp.stack(even, 1), jnp.stack(odd, 1)], 1)
    query_grad[...] = both.reshape(TOKENS, PLANES * 8, HEAD_DIM).astype(BF16)


def merge(place, keep, got):
    return pl.pallas_call(
        merge_kernel,
        out_shape=array(TOKENS, PLANES * 8, HEAD_DIM),
        in_specs=[IN_SMEM, IN_VMEM, IN_VMEM],
        out_specs=IN_VMEM,
        compiler_params=pltpu.CompilerParams(vmem_limit_bytes=VMEM_LIMIT),
        name="merge_heads",
    )(place, keep, got)


def sum_kernel(rows, terms, key_grad, value_grad, key_sum, value_sum):
    key_sum[...] = jnp.zeros_like(key_sum)
    value_sum[...] = jnp.zeros_like(value_sum)

    def add(index, carry):
        row = wanted_row(rows, index)

        @pl.when(row >= 0)
        def _():
            key_sum[row] += terms[index, 0].astype(F32)
            value_sum[row] += terms[index, 1].astype(F32)

        return carry

    lax.fori_loop(0, CTX, add, 0)
    key_grad[...] = key_sum[...].astype(BF16)
    value_grad[...] = value_sum[...].astype(BF16)


def owner_sum(rows, terms):
    grad = array(OWNED, BLOCK, HEAD_DIM)
    return pl.pallas_call(
        sum_kernel,
        out_shape=(grad, grad),
        in_specs=[IN_SMEM, IN_VMEM],
        out_specs=(IN_VMEM, IN_VMEM),
        scratch_shapes=[pltpu.VMEM((OWNED, BLOCK, HEAD_DIM), F32)] * 2,
        compiler_params=pltpu.CompilerParams(vmem_limit_bytes=VMEM_LIMIT),
        name="owner_sum",
    )(rows, terms)


def exchange(blocks):
    return lax.all_to_all(blocks, "ctx", split_axis=0, concat_axis=0, tiled=True)


def swap_partner(array):
    return lax.ppermute(array, "head", [(i, i ^ 1) for i in range(PLANES * CORES)])


def along_planes(parcels):
    moved = [parcels[0]]
    for shift in range(1, PLANES):
        pairs = [(i, (i + shift * CORES) % (PLANES * CORES)) for i in range(PLANES * CORES)]
        moved.append(lax.ppermute(parcels[shift], "head", pairs))
    return moved


def per_device(queries, keys, values, out_grad, selected):
    ctx, head = lax.axis_index("ctx"), lax.axis_index("head")
    place = jnp.stack([ctx, head >> 1, head & 1]).astype(jnp.int32)
    table = selected[0].T
    slots = lax.dynamic_slice_in_dim(table, ctx * QBLOCKS, QBLOCKS, 1) // OWNED
    blocks = (OWNED, BLOCK, HEAD_DIM)
    packed, rows = pack(place, table, keys.reshape(blocks), values.reshape(blocks))
    fetched = exchange(packed)
    keep, send = split(place, rows, queries, out_grad)
    parcels = along_planes(join(keep, swap_partner(send)))
    terms, *results = attend_backward(place, slots, fetched, parcels)
    back = exchange(terms)
    keep, send = swap(place, along_planes(results))
    query_grad = merge(place, keep, swap_partner(send))
    key_grad, value_grad = owner_sum(rows, back)
    return query_grad, key_grad.reshape(keys.shape), value_grad.reshape(values.shape)


def solution(mesh):
    tokens = P(("ctx", "head"), None, None)
    context = P("ctx", "head", None)
    return jax.shard_map(
        per_device,
        mesh=mesh,
        in_specs=(tokens, context, context, tokens, P("head", None, None)),
        out_specs=(tokens, context, context),
        check_vma=False,
    )
```

time: 207 us -> 148 us (0.71)
  the two profiles are of different devices: /device:TPU:126 before, /device:TPU:666 now
where the time goes in v2:
time: 148 us; the launch traced here: 147 us
  starting transfers between devices  82.9 us (56%)
  waiting for transfers between devices  45.9 us (31%)
  Pallas kernels  16.6 us (11%)
    ppermute x14, starting transfers between devices, along_planes(): moved.append(lax.ppermute(parcels[shift], 'head', pairs))  56.4 us
    all_to_all x2, waiting for transfers between devices, exchange(): lax.all_to_all(blocks, 'ctx', split_axis=0, concat_axis=0, tiled=True)  40.1 us
    all_to_all x2, starting transfers between devices, exchange(): lax.all_to_all(blocks, 'ctx', split_axis=0, concat_axis=0, tiled=True)  22.7 us
    pallas_call x1, Pallas kernels, attend_backward(): pl.pallas_call(attend_kernel, out_shape=(array(CTX, 2, BLOCK, HEAD_DIM),)...  6.98 us
    pallas_call x1, Pallas kernels, pack(): pl.pallas_call(pack_kernel, out_shape=(array(CTX, 2, BLOCK, HEAD_DIM), ar...  3.92 us
    ppermute x2, starting transfers between devices, swap_partner(): lax.ppermute(array, 'head', [(i, i ^ 1) for i in range(PLANES * CORES)])  3.84 us
    pallas_call x1, Pallas kernels, owner_sum(): pl.pallas_call(sum_kernel, out_shape=(grad, grad), in_specs=[IN_SMEM, IN_...  3.18 us
    ppermute x14, waiting for transfers between devices, along_planes(): moved.append(lax.ppermute(parcels[shift], 'head', pairs))  3.1 us
  transfers between devices with their start and end apart: 18, of which 8 were waited for; matrix products, arithmetic and copies ran while one was open for 0% of the time, Pallas kernels for 2%

profile of v2, /device:TPU:666, one launch (start us, length us, event | category | flops | bytes accessed | tf_op | source)
XLA Modules:
  0.0 147.1 jit_solution(7545931559652219042)
XLA Ops:
  0.6 0.6 pad_add_fusion.place
  1.2 3.9 %pack_blocks.1 = (bf16[64,2,64,128]{3,2,1,0:T(8,128)(2,1)}, s32[1,192]{1,0:T(1,128)}) custom-call(s32[3]{0:T(128)} %pad_add_fusion.place, s32[16,192]{1,0:T(8,128)} %bitcast.30, bf16[32,64,128]{2,1,0:T(8,128)(2,1)} %bitcast.28, bf16[32,64,128]{2,1,0:T(8,128)(2,1)} %bitcast.29), custom_call_target="tpu_custom_call" | custom-call | tf_op jit(solution)/shard_map/pack_blocks/pallas_call | solution.py:82
  5.1 0.0 copy-start
  5.2 0.0 copy-start.1
  5.2 0.0 copy-start.3
  5.2 0.0 copy-start.4
  5.2 13.7 %all-to-all-start = ((bf16[64,2,64,128]{3,2,1,0:T(8,128)(2,1)}), bf16[64,2,64,128]{3,2,1,0:T(8,128)(2,1)}, u32[]{:S(2)}, u32[]{:S(2)}) async-start(bf16[64,2,64,128]{3,2,1,0:T(8,128)(2,1)} %get-tuple-element.28), calls=%async_computation | async-start | bytes 4194304 | tf_op jit(solution)/shard_map/all_to_all | solution.py:323
  19.0 0.7 split_heads.1
  19.7 1.9 %collective-permute-start = (bf16[8,2,48,128]{3,2,1,0:T(8,128)(2,1)S(1)}, bf16[8,2,48,128]{3,2,1,0:T(8,128)(2,1)S(1)}, u32[]{:S(2)}, u32[]{:S(2)}) collective-permute-start(bf16[8,2,48,128]{3,2,1,0:T(8,128)(2,1)S(1)} %get-tuple-element.31), channel_id=1, source_target_pairs={{0,1},{1,0},{2,3},{3,2},{4,5},{5,4},{6,7},{7,6},{8,9},{9,8},{10,11... | collective-permute-start | bytes 589832 | tf_op jit(solution)/shard_map/ppermute | solution.py:327
  21.6 1.4 collective-permute-done.got
  23.0 4.3 %collective-permute-start.1 = (bf16[4,48,128]{2,1,0:T(8,128)(2,1)S(1)}, bf16[4,48,128]{2,1,0:T(8,128)(2,1)S(1)}, u32[]{:S(2)}, u32[]{:S(2)}) collective-permute-start(bf16[4,48,128]{2,1,0:T(8,128)(2,1)S(1)} %get-tuple-element.33), channel_id=1, source_target_pairs={{0,2},{1,3},{2,4},{3,5},{4,6},{5,7},{6,8},{7,9},{8,10},{9,11},{10,... | collective-permute-start | bytes 147464 | tf_op jit(solution)/shard_map/ppermute | solution.py:334
  27.3 3.7 %collective-permute-start.2 = (bf16[4,48,128]{2,1,0:T(8,128)(2,1)S(1)}, bf16[4,48,128]{2,1,0:T(8,128)(2,1)S(1)}, u32[]{:S(2)}, u32[]{:S(2)}) collective-permute-start(bf16[4,48,128]{2,1,0:T(8,128)(2,1)S(1)} %get-tuple-element.34), channel_id=1, source_target_pairs={{0,4},{1,5},{2,6},{3,7},{4,8},{5,9},{6,10},{7,11},{8,12},{9,13},{1... | collective-permute-start | bytes 147464 | tf_op jit(solution)/shard_map/ppermute | solution.py:334
  31.1 1.9 %collective-permute-start.3 = (bf16[4,48,128]{2,1,0:T(8,128)(2,1)S(1)}, bf16[4,48,128]{2,1,0:T(8,128)(2,1)S(1)}, u32[]{:S(2)}, u32[]{:S(2)}) collective-permute-start(bf16[4,48,128]{2,1,0:T(8,128)(2,1)S(1)} %get-tuple-element.35), channel_id=1, source_target_pairs={{0,6},{1,7},{2,8},{3,9},{4,10},{5,11},{6,12},{7,13},{8,14},{9,15},... | collective-permute-start | bytes 147464 | tf_op jit(solution)/shard_map/ppermute | solution.py:334
  33.0 8.4 %collective-permute-start.4 = (bf16[4,48,128]{2,1,0:T(8,128)(2,1)S(1)}, bf16[4,48,128]{2,1,0:T(8,128)(2,1)S(1)}, u32[]{:S(2)}, u32[]{:S(2)}) collective-permute-start(bf16[4,48,128]{2,1,0:T(8,128)(2,1)S(1)} %get-tuple-element.36), channel_id=1, source_target_pairs={{0,8},{1,9},{2,10},{3,11},{4,12},{5,13},{6,14},{7,15},{8,0},{9,1},... | collective-permute-start | bytes 147464 | tf_op jit(solution)/shard_map/ppermute | solution.py:334
  41.4 1.9 %collective-permute-start.5 = (bf16[4,48,128]{2,1,0:T(8,128)(2,1)S(1)}, bf16[4,48,128]{2,1,0:T(8,128)(2,1)S(1)}, u32[]{:S(2)}, u32[]{:S(2)}) collective-permute-start(bf16[4,48,128]{2,1,0:T(8,128)(2,1)S(1)} %get-tuple-element.37), channel_id=1, source_target_pairs={{0,10},{1,11},{2,12},{3,13},{4,14},{5,15},{6,0},{7,1},{8,2},{9,3},... | collective-permute-start | bytes 147464 | tf_op jit(solution)/shard_map/ppermute | solution.py:334
  43.3 0.0 collective-permute-done.1.refs_1_
  43.3 3.4 %collective-permute-start.6 = (bf16[4,48,128]{2,1,0:T(8,128)(2,1)S(1)}, bf16[4,48,128]{2,1,0:T(8,128)(2,1)S(1)}, u32[]{:S(2)}, u32[]{:S(2)}) collective-permute-start(bf16[4,48,128]{2,1,0:T(8,128)(2,1)S(1)} %get-tuple-element.38), channel_id=1, source_target_pairs={{0,12},{1,13},{2,14},{3,15},{4,0},{5,1},{6,2},{7,3},{8,4},{9,5},{1... | collective-permute-start | bytes 147464 | tf_op jit(solution)/shard_map/ppermute | solution.py:334
  46.7 0.0 collective-permute-done.2.refs_2_
  46.7 4.6 %collective-permute-start.7 = (bf16[4,48,128]{2,1,0:T(8,128)(2,1)S(1)}, bf16[4,48,128]{2,1,0:T(8,128)(2,1)S(1)}, u32[]{:S(2)}, u32[]{:S(2)}) collective-permute-start(bf16[4,48,128]{2,1,0:T(8,128)(2,1)S(1)} %get-tuple-element.39), channel_id=1, source_target_pairs={{0,14},{1,15},{2,0},{3,1},{4,2},{5,3},{6,4},{7,5},{8,6},{9,7},{10,... | collective-permute-start | bytes 147464 | tf_op jit(solution)/shard_map/ppermute | solution.py:334
  51.3 0.1 add_select_fusion.slots
  51.4 0.0 collective-permute-done.3.refs_3_
  51.4 0.0 collective-permute-done.4.refs_4_
  51.4 0.7 collective-permute-done.5.refs_5_
  52.1 0.3 collective-permute-done.6.refs_6_
  52.5 0.6 collective-permute-done.7.refs_7_
  53.0 20.1 %all-to-all-done.fetched = bf16[64,2,64,128]{3,2,1,0:T(8,128)(2,1)} async-done(((bf16[64,2,64,128]{3,2,1,0:T(8,128)(2,1)}), bf16[64,2,64,128]{3,2,1,0:T(8,128)(2,1)}, u32[]{:S(2)}, u32[]{:S(2)}) %all-to-all-start) | async-done | bytes 2097184 | tf_op jit(solution)/shard_map/all_to_all | solution.py:323
  73.1 7.0 %attend_backward.1 = (bf16[64,2,64,128]{3,2,1,0:T(8,128)(2,1)}, bf16[2,48,128]{2,1,0:T(8,128)(2,1)S(1)}, bf16[2,48,128]{2,1,0:T(8,128)(2,1)S(1)}, bf16[2,48,128]...) custom-call(s32[3]{0:T(128)S(1)} %copy-done.2, ...), custom_call_target="tpu_custom_call" | custom-call | tf_op jit(solution)/shard_map/attend_backward/pallas_call | solution.py:223
  80.1 9.0 %all-to-all-start.1 = ((bf16[64,2,64,128]{3,2,1,0:T(8,128)(2,1)}), bf16[64,2,64,128]{3,2,1,0:T(8,128)(2,1)S(1)}, u32[]{:S(2)}, u32[]{:S(2)}) async-start(bf16[64,2,64,128]{3,2,1,0:T(8,128)(2,1)} %get-tuple-element.50), calls=%async_computation.1 | async-start | bytes 4194304 | tf_op jit(solution)/shard_map/all_to_all | solution.py:323
  89.1 4.2 %collective-permute-start.8 = (bf16[2,48,128]{2,1,0:T(8,128)(2,1)S(1)}, bf16[2,48,128]{2,1,0:T(8,128)(2,1)S(1)}, u32[]{:S(2)}, u32[]{:S(2)}) collective-permute-start(bf16[2,48,128]{2,1,0:T(8,128)(2,1)S(1)} %get-tuple-element.41), channel_id=1, source_target_pairs={{0,2},{1,3},{2,4},{3,5},{4,6},{5,7},{6,8},{7,9},{8,10},{9,11},{10,... | collective-permute-start | bytes 73736 | tf_op jit(solution)/shard_map/ppermute | solution.py:334
  93.3 3.8 %collective-permute-start.9 = (bf16[2,48,128]{2,1,0:T(8,128)(2,1)S(1)}, bf16[2,48,128]{2,1,0:T(8,128)(2,1)S(1)}, u32[]{:S(2)}, u32[]{:S(2)}) collective-permute-start(bf16[2,48,128]{2,1,0:T(8,128)(2,1)S(1)} %get-tuple-element.42), channel_id=1, source_target_pairs={{0,4},{1,5},{2,6},{3,7},{4,8},{5,9},{6,10},{7,11},{8,12},{9,13},{1... | collective-permute-start | bytes 73736 | tf_op jit(solution)/shard_map/ppermute | solution.py:334
  97.1 1.9 %collective-permute-start.10 = (bf16[2,48,128]{2,1,0:T(8,128)(2,1)S(1)}, bf16[2,48,128]{2,1,0:T(8,128)(2,1)S(1)}, u32[]{:S(2)}, u32[]{:S(2)}) collective-permute-start(bf16[2,48,128]{2,1,0:T(8,128)(2,1)S(1)} %get-tuple-element.43), channel_id=1, source_target_pairs={{0,6},{1,7},{2,8},{3,9},{4,10},{5,11},{6,12},{7,13},{8,14},{9,15},... | collective-permute-start | bytes 73736 | tf_op jit(solution)/shard_map/ppermute | solution.py:334
  99.0 8.4 %collective-permute-start.11 = (bf16[2,48,128]{2,1,0:T(8,128)(2,1)S(1)}, bf16[2,48,128]{2,1,0:T(8,128)(2,1)S(1)}, u32[]{:S(2)}, u32[]{:S(2)}) collective-permute-start(bf16[2,48,128]{2,1,0:T(8,128)(2,1)S(1)} %get-tuple-element.44), channel_id=1, source_target_pairs={{0,8},{1,9},{2,10},{3,11},{4,12},{5,13},{6,14},{7,15},{8,0},{9,1},... | collective-permute-start | bytes 73736 | tf_op jit(solution)/shard_map/ppermute | solution.py:334
  107.4 1.9 %collective-permute-start.12 = (bf16[2,48,128]{2,1,0:T(8,128)(2,1)S(1)}, bf16[2,48,128]{2,1,0:T(8,128)(2,1)S(1)}, u32[]{:S(2)}, u32[]{:S(2)}) collective-permute-start(bf16[2,48,128]{2,1,0:T(8,128)(2,1)S(1)} %get-tuple-element.45), channel_id=1, source_target_pairs={{0,10},{1,11},{2,12},{3,13},{4,14},{5,15},{6,0},{7,1},{8,2},{9,3},... | collective-permute-start | bytes 73736 | tf_op jit(solution)/shard_map/ppermute | solution.py:334
  109.3 0.0 collective-permute-done.8.refs_1_
  109.4 3.4 %collective-permute-start.13 = (bf16[2,48,128]{2,1,0:T(8,128)(2,1)S(1)}, bf16[2,48,128]{2,1,0:T(8,128)(2,1)S(1)}, u32[]{:S(2)}, u32[]{:S(2)}) collective-permute-start(bf16[2,48,128]{2,1,0:T(8,128)(2,1)S(1)} %get-tuple-element.46), channel_id=1, source_target_pairs={{0,12},{1,13},{2,14},{3,15},{4,0},{5,1},{6,2},{7,3},{8,4},{9,5},{1... | collective-permute-start | bytes 73736 | tf_op jit(solution)/shard_map/ppermute | solution.py:334
  112.7 0.0 collective-permute-done.9.refs_2_
  112.7 4.6 %collective-permute-start.14 = (bf16[2,48,128]{2,1,0:T(8,128)(2,1)S(1)}, bf16[2,48,128]{2,1,0:T(8,128)(2,1)S(1)}, u32[]{:S(2)}, u32[]{:S(2)}) collective-permute-start(bf16[2,48,128]{2,1,0:T(8,128)(2,1)S(1)} %get-tuple-element.47), channel_id=1, source_target_pairs={{0,14},{1,15},{2,0},{3,1},{4,2},{5,3},{6,4},{7,5},{8,6},{9,7},{10,... | collective-permute-start | bytes 73736 | tf_op jit(solution)/shard_map/ppermute | solution.py:334
  117.3 0.0 collective-permute-done.10.refs_3_
  117.3 0.0 collective-permute-done.11.refs_4_
  117.4 0.0 collective-permute-done.12.refs_5_
  117.4 0.0 collective-permute-done.13.refs_6_
  117.4 1.5 collective-permute-done.14.refs_7_
  118.8 0.6 swap_cores.1
  119.4 1.9 %collective-permute-start.15 = (bf16[8,48,128]{2,1,0:T(8,128)(2,1)S(1)}, bf16[8,48,128]{2,1,0:T(8,128)(2,1)S(1)}, u32[]{:S(2)}, u32[]{:S(2)}) collective-permute-start(bf16[8,48,128]{2,1,0:T(8,128)(2,1)S(1)} %get-tuple-element.49), channel_id=1, source_target_pairs={{0,1},{1,0},{2,3},{3,2},{4,5},{5,4},{6,7},{7,6},{8,9},{9,8},{10,11... | collective-permute-start | bytes 294920 | tf_op jit(solution)/shard_map/ppermute | solution.py:327
  121.3 1.3 collective-permute-done.15.got
  122.6 1.3 merge_heads.1
  123.9 20.1 %all-to-all-done.1.terms = bf16[64,2,64,128]{3,2,1,0:T(8,128)(2,1)S(1)} async-done(((bf16[64,2,64,128]{3,2,1,0:T(8,128)(2,1)}), bf16[64,2,64,128]{3,2,1,0:T(8,128)(2,1)S(1)}, u32[]{:S(2)}, u32[]{:S(2)}) %all-to-all-start.1) | async-done | bytes 2097184 | tf_op jit(solution)/shard_map/all_to_all | solution.py:323
  144.0 3.2 %owner_sum.1 = (bf16[32,64,128]{2,1,0:T(8,128)(2,1)}, bf16[32,64,128]{2,1,0:T(8,128)(2,1)}) custom-call(s32[1,192]{1,0:T(1,128)S(1)} %copy-done.3, bf16[64,2,64,128]{3,2,1,0:T(8,128)(2,1)S(1)} %all-to-all-done.1.terms), custom_call_target="tpu_custom_call" | custom-call | tf_op jit(solution)/shard_map/owner_sum/pallas_call | solution.py:311
  (7 shorter events, 0.0 us)
Async XLA Ops:
  5.1 13.8 %copy-start = (bf16[12,64,128]{2,1,0:T(8,128)(2,1)S(1)}, bf16[12,64,128]{2,1,0:T(8,128)(2,1)}, u32[]{:S(2)}) copy-start(bf16[12,64,128]{2,1,0:T(8,128)(2,1)} %queries.1) | copy-start | bytes 589828
  5.2 13.8 %copy-start.1 = (bf16[12,64,128]{2,1,0:T(8,128)(2,1)S(1)}, bf16[12,64,128]{2,1,0:T(8,128)(2,1)}, u32[]{:S(2)}) copy-start(bf16[12,64,128]{2,1,0:T(8,128)(2,1)} %grads.1) | copy-start | bytes 589828
  5.2 13.8 %copy-start.2 = (s32[3]{0:T(128)S(1)}, s32[3]{0:T(128)}, u32[]{:S(2)}) copy-start(s32[3]{0:T(128)} %pad_add_fusion.place) | copy-start | bytes 40
  5.2 13.8 %copy-start.3 = (s32[1,192]{1,0:T(1,128)S(1)}, s32[1,192]{1,0:T(1,128)}, u32[]{:S(2)}) copy-start(s32[1,192]{1,0:T(1,128)} %get-tuple-element.29.rows) | copy-start | bytes 2308
  5.2 46.1 %copy-start.4 = (s32[1,192,16]{1,2,0:T(8,128)S(1)}, s32[1,192,16]{1,2,0:T(8,128)}, u32[]{:S(2)}) copy-start(s32[1,192,16]{1,2,0:T(8,128)} %param.9) | copy-start | bytes 36868
  5.2 67.9 %all-to-all-start = ((bf16[64,2,64,128]{3,2,1,0:T(8,128)(2,1)}), bf16[64,2,64,128]{3,2,1,0:T(8,128)(2,1)}, u32[]{:S(2)}, u32[]{:S(2)}) async-start(bf16[64,2,64,128]{3,2,1,0:T(8,128)(2,1)} %get-tuple-element.28), calls=%async_computation | async-start | bytes 4194304 | tf_op jit(solution)/shard_map/all_to_all | solution.py:323
  19.7 3.3 %collective-permute-start = (bf16[8,2,48,128]{3,2,1,0:T(8,128)(2,1)S(1)}, bf16[8,2,48,128]{3,2,1,0:T(8,128)(2,1)S(1)}, u32[]{:S(2)}, u32[]{:S(2)}) collective-permute-start(bf16[8,2,48,128]{3,2,1,0:T(8,128)(2,1)S(1)} %get-tuple-element.31), channel_id=1, source_target_pairs={{0,1},{1,0},{2,3},{3,2},{4,5},{5,4},{6,7},{7,6},{8,9},{9,8},{10,11... | collective-permute-start | bytes 589832 | tf_op jit(solution)/shard_map/ppermute | solution.py:327
  23.0 20.3 %collective-permute-start.1 = (bf16[4,48,128]{2,1,0:T(8,128)(2,1)S(1)}, bf16[4,48,128]{2,1,0:T(8,128)(2,1)S(1)}, u32[]{:S(2)}, u32[]{:S(2)}) collective-permute-start(bf16[4,48,128]{2,1,0:T(8,128)(2,1)S(1)} %get-tuple-element.33), channel_id=1, source_target_pairs={{0,2},{1,3},{2,4},{3,5},{4,6},{5,7},{6,8},{7,9},{8,10},{9,11},{10,... | collective-permute-start | bytes 147464 | tf_op jit(solution)/shard_map/ppermute | solution.py:334
  27.3 19.4 %collective-permute-start.2 = (bf16[4,48,128]{2,1,0:T(8,128)(2,1)S(1)}, bf16[4,48,128]{2,1,0:T(8,128)(2,1)S(1)}, u32[]{:S(2)}, u32[]{:S(2)}) collective-permute-start(bf16[4,48,128]{2,1,0:T(8,128)(2,1)S(1)} %get-tuple-element.34), channel_id=1, source_target_pairs={{0,4},{1,5},{2,6},{3,7},{4,8},{5,9},{6,10},{7,11},{8,12},{9,13},{1... | collective-permute-start | bytes 147464 | tf_op jit(solution)/shard_map/ppermute | solution.py:334
  31.1 20.3 %collective-permute-start.3 = (bf16[4,48,128]{2,1,0:T(8,128)(2,1)S(1)}, bf16[4,48,128]{2,1,0:T(8,128)(2,1)S(1)}, u32[]{:S(2)}, u32[]{:S(2)}) collective-permute-start(bf16[4,48,128]{2,1,0:T(8,128)(2,1)S(1)} %get-tuple-element.35), channel_id=1, source_target_pairs={{0,6},{1,7},{2,8},{3,9},{4,10},{5,11},{6,12},{7,13},{8,14},{9,15},... | collective-permute-start | bytes 147464 | tf_op jit(solution)/shard_map/ppermute | solution.py:334
  33.0 18.4 %collective-permute-start.4 = (bf16[4,48,128]{2,1,0:T(8,128)(2,1)S(1)}, bf16[4,48,128]{2,1,0:T(8,128)(2,1)S(1)}, u32[]{:S(2)}, u32[]{:S(2)}) collective-permute-start(bf16[4,48,128]{2,1,0:T(8,128)(2,1)S(1)} %get-tuple-element.36), channel_id=1, source_target_pairs={{0,8},{1,9},{2,10},{3,11},{4,12},{5,13},{6,14},{7,15},{8,0},{9,1},... | collective-permute-start | bytes 147464 | tf_op jit(solution)/shard_map/ppermute | solution.py:334
  41.4 10.7 %collective-permute-start.5 = (bf16[4,48,128]{2,1,0:T(8,128)(2,1)S(1)}, bf16[4,48,128]{2,1,0:T(8,128)(2,1)S(1)}, u32[]{:S(2)}, u32[]{:S(2)}) collective-permute-start(bf16[4,48,128]{2,1,0:T(8,128)(2,1)S(1)} %get-tuple-element.37), channel_id=1, source_target_pairs={{0,10},{1,11},{2,12},{3,13},{4,14},{5,15},{6,0},{7,1},{8,2},{9,3},... | collective-permute-start | bytes 147464 | tf_op jit(solution)/shard_map/ppermute | solution.py:334
  43.3 9.1 %collective-permute-start.6 = (bf16[4,48,128]{2,1,0:T(8,128)(2,1)S(1)}, bf16[4,48,128]{2,1,0:T(8,128)(2,1)S(1)}, u32[]{:S(2)}, u32[]{:S(2)}) collective-permute-start(bf16[4,48,128]{2,1,0:T(8,128)(2,1)S(1)} %get-tuple-element.38), channel_id=1, source_target_pairs={{0,12},{1,13},{2,14},{3,15},{4,0},{5,1},{6,2},{7,3},{8,4},{9,5},{1... | collective-permute-start | bytes 147464 | tf_op jit(solution)/shard_map/ppermute | solution.py:334
  46.7 6.3 %collective-permute-start.7 = (bf16[4,48,128]{2,1,0:T(8,128)(2,1)S(1)}, bf16[4,48,128]{2,1,0:T(8,128)(2,1)S(1)}, u32[]{:S(2)}, u32[]{:S(2)}) collective-permute-start(bf16[4,48,128]{2,1,0:T(8,128)(2,1)S(1)} %get-tuple-element.39), channel_id=1, source_target_pairs={{0,14},{1,15},{2,0},{3,1},{4,2},{5,3},{6,4},{7,5},{8,6},{9,7},{10,... | collective-permute-start | bytes 147464 | tf_op jit(solution)/shard_map/ppermute | solution.py:334
  80.1 63.9 %all-to-all-start.1 = ((bf16[64,2,64,128]{3,2,1,0:T(8,128)(2,1)}), bf16[64,2,64,128]{3,2,1,0:T(8,128)(2,1)S(1)}, u32[]{:S(2)}, u32[]{:S(2)}) async-start(bf16[64,2,64,128]{3,2,1,0:T(8,128)(2,1)} %get-tuple-element.50), calls=%async_computation.1 | async-start | bytes 4194304 | tf_op jit(solution)/shard_map/all_to_all | solution.py:323
  89.1 20.3 %collective-permute-start.8 = (bf16[2,48,128]{2,1,0:T(8,128)(2,1)S(1)}, bf16[2,48,128]{2,1,0:T(8,128)(2,1)S(1)}, u32[]{:S(2)}, u32[]{:S(2)}) collective-permute-start(bf16[2,48,128]{2,1,0:T(8,128)(2,1)S(1)} %get-tuple-element.41), channel_id=1, source_target_pairs={{0,2},{1,3},{2,4},{3,5},{4,6},{5,7},{6,8},{7,9},{8,10},{9,11},{10,... | collective-permute-start | bytes 73736 | tf_op jit(solution)/shard_map/ppermute | solution.py:334
  93.3 19.4 %collective-permute-start.9 = (bf16[2,48,128]{2,1,0:T(8,128)(2,1)S(1)}, bf16[2,48,128]{2,1,0:T(8,128)(2,1)S(1)}, u32[]{:S(2)}, u32[]{:S(2)}) collective-permute-start(bf16[2,48,128]{2,1,0:T(8,128)(2,1)S(1)} %get-tuple-element.42), channel_id=1, source_target_pairs={{0,4},{1,5},{2,6},{3,7},{4,8},{5,9},{6,10},{7,11},{8,12},{9,13},{1... | collective-permute-start | bytes 73736 | tf_op jit(solution)/shard_map/ppermute | solution.py:334
  97.1 20.2 %collective-permute-start.10 = (bf16[2,48,128]{2,1,0:T(8,128)(2,1)S(1)}, bf16[2,48,128]{2,1,0:T(8,128)(2,1)S(1)}, u32[]{:S(2)}, u32[]{:S(2)}) collective-permute-start(bf16[2,48,128]{2,1,0:T(8,128)(2,1)S(1)} %get-tuple-element.43), channel_id=1, source_target_pairs={{0,6},{1,7},{2,8},{3,9},{4,10},{5,11},{6,12},{7,13},{8,14},{9,15},... | collective-permute-start | bytes 73736 | tf_op jit(solution)/shard_map/ppermute | solution.py:334
  99.0 18.3 %collective-permute-start.11 = (bf16[2,48,128]{2,1,0:T(8,128)(2,1)S(1)}, bf16[2,48,128]{2,1,0:T(8,128)(2,1)S(1)}, u32[]{:S(2)}, u32[]{:S(2)}) collective-permute-start(bf16[2,48,128]{2,1,0:T(8,128)(2,1)S(1)} %get-tuple-element.44), channel_id=1, source_target_pairs={{0,8},{1,9},{2,10},{3,11},{4,12},{5,13},{6,14},{7,15},{8,0},{9,1},... | collective-permute-start | bytes 73736 | tf_op jit(solution)/shard_map/ppermute | solution.py:334
  107.4 9.9 %collective-permute-start.12 = (bf16[2,48,128]{2,1,0:T(8,128)(2,1)S(1)}, bf16[2,48,128]{2,1,0:T(8,128)(2,1)S(1)}, u32[]{:S(2)}, u32[]{:S(2)}) collective-permute-start(bf16[2,48,128]{2,1,0:T(8,128)(2,1)S(1)} %get-tuple-element.45), channel_id=1, source_target_pairs={{0,10},{1,11},{2,12},{3,13},{4,14},{5,15},{6,0},{7,1},{8,2},{9,3},... | collective-permute-start | bytes 73736 | tf_op jit(solution)/shard_map/ppermute | solution.py:334
  109.4 8.0 %collective-permute-start.13 = (bf16[2,48,128]{2,1,0:T(8,128)(2,1)S(1)}, bf16[2,48,128]{2,1,0:T(8,128)(2,1)S(1)}, u32[]{:S(2)}, u32[]{:S(2)}) collective-permute-start(bf16[2,48,128]{2,1,0:T(8,128)(2,1)S(1)} %get-tuple-element.46), channel_id=1, source_target_pairs={{0,12},{1,13},{2,14},{3,15},{4,0},{5,1},{6,2},{7,3},{8,4},{9,5},{1... | collective-permute-start | bytes 73736 | tf_op jit(solution)/shard_map/ppermute | solution.py:334
  112.7 6.1 %collective-permute-start.14 = (bf16[2,48,128]{2,1,0:T(8,128)(2,1)S(1)}, bf16[2,48,128]{2,1,0:T(8,128)(2,1)S(1)}, u32[]{:S(2)}, u32[]{:S(2)}) collective-permute-start(bf16[2,48,128]{2,1,0:T(8,128)(2,1)S(1)} %get-tuple-element.47), channel_id=1, source_target_pairs={{0,14},{1,15},{2,0},{3,1},{4,2},{5,3},{6,4},{7,5},{8,6},{9,7},{10,... | collective-permute-start | bytes 73736 | tf_op jit(solution)/shard_map/ppermute | solution.py:334
  119.4 3.2 %collective-permute-start.15 = (bf16[8,48,128]{2,1,0:T(8,128)(2,1)S(1)}, bf16[8,48,128]{2,1,0:T(8,128)(2,1)S(1)}, u32[]{:S(2)}, u32[]{:S(2)}) collective-permute-start(bf16[8,48,128]{2,1,0:T(8,128)(2,1)S(1)} %get-tuple-element.49), channel_id=1, source_target_pairs={{0,1},{1,0},{2,3},{3,2},{4,5},{5,4},{6,7},{7,6},{8,9},{9,8},{10,11... | collective-permute-start | bytes 294920 | tf_op jit(solution)/shard_map/ppermute | solution.py:327

commit v3 on v2

v3 whole, which is shorter than its diff:
```python
import functools

import jax
import jax.numpy as jnp
from jax import lax
from jax.experimental import pallas as pl
from jax.experimental.pallas import tpu as pltpu
from jax.sharding import PartitionSpec as P

BLOCK = 64
SELECTED = 16
CTX = 64
OWNED = 32
QBLOCKS = 3
QBLOCKS_ALL = 192
HEAD_DIM = 128
GROUP_HEADS = 4
ROWS = BLOCK * GROUP_HEADS
KEYS = SELECTED * BLOCK
TOKENS = 12
PIECE = TOKENS * GROUP_HEADS
PLANES = 8
CHUNK = 256
CORES = 2
SCALE = HEAD_DIM**-0.5
LOG2E = 1.4426950408889634
VMEM_LIMIT = 40 * 1024 * 1024
VMEM_ALL = 62 * 1024 * 1024
VMEM_ATTEND = 44 * 1024 * 1024
BF16 = jnp.bfloat16
F32 = jnp.float32
IN_VMEM = pl.BlockSpec(memory_space=pltpu.VMEM)
IN_SMEM = pl.BlockSpec(memory_space=pltpu.SMEM)
IN_HBM = pl.BlockSpec(memory_space=pltpu.HBM)


def array(*shape, dtype=BF16):
    return jax.ShapeDtypeStruct(shape, dtype)


def wanted_row(rows, index):
    first = rows[0, QBLOCKS * index]
    return jnp.maximum(jnp.maximum(first, rows[0, QBLOCKS * index + 1]), rows[0, QBLOCKS * index + 2])


def pack_kernel(table, keys, values, packed, rows, key_buf, value_buf, out_buf, table_buf, row_buf, in_sems, out_sems):
    picked = pltpu.make_async_copy(table, table_buf, in_sems.at[0])
    loads = [
        pltpu.make_async_copy(keys, key_buf, in_sems.at[1]),
        pltpu.make_async_copy(values, value_buf, in_sems.at[2]),
    ]
    picked.start()
    for load in loads:
        load.start()
    picked.wait()
    picks = table_buf[...]
    mine = jnp.where(picks // OWNED == lax.axis_index("ctx"), picks % OWNED, -1)
    row_buf[...] = jnp.max(mine, axis=0, keepdims=True)
    to_scalars = pltpu.make_async_copy(row_buf, rows, in_sems.at[3])
    to_scalars.start()
    to_scalars.wait()
    for load in loads:
        load.wait()
    parts = out_sems.shape[0]
    size = CTX // parts

    def store(part):
        span = pl.ds(part * size, size)
        return pltpu.make_async_copy(out_buf.at[span], packed.at[span], out_sems.at[part])

    for part in range(parts):

        def copy(index, carry):
            row = jnp.maximum(wanted_row(rows, index), 0)
            out_buf[index, 0] = key_buf[row]
            out_buf[index, 1] = value_buf[row]
            return carry

        lax.fori_loop(part * size, (part + 1) * size, copy, 0, unroll=4)
        store(part).start()
    for part in range(parts):
        store(part).wait()


def pack(table, keys, values):
    return pl.pallas_call(
        pack_kernel,
        out_shape=(array(CTX, 2, BLOCK, HEAD_DIM), array(1, QBLOCKS_ALL, dtype=jnp.int32)),
        in_specs=[IN_HBM, IN_HBM, IN_HBM],
        out_specs=(IN_HBM, IN_SMEM),
        scratch_shapes=[
            pltpu.VMEM((OWNED, BLOCK, HEAD_DIM), BF16),
            pltpu.VMEM((OWNED, BLOCK, HEAD_DIM), BF16),
            pltpu.VMEM((CTX, 2, BLOCK, HEAD_DIM), BF16),
            pltpu.VMEM((SELECTED, QBLOCKS_ALL), jnp.int32),
            pltpu.VMEM((1, QBLOCKS_ALL), jnp.int32),
            pltpu.SemaphoreType.DMA((4,)),
            pltpu.SemaphoreType.DMA((8,)),
        ],
        compiler_params=pltpu.CompilerParams(vmem_limit_bytes=VMEM_ALL),
        name="pack_blocks",
    )(table, keys, values)


def halves(first, second):
    low = lax.broadcasted_iota(jnp.int32, first.shape, first.ndim - 2) < GROUP_HEADS
    axis = first.ndim - 2
    return (
        jnp.where(low, first, pltpu.roll(second, GROUP_HEADS, axis)),
        jnp.where(low, pltpu.roll(first, GROUP_HEADS, axis), second),
    )


def split_kernel(rows, queries, grads, keep, send):
    head = lax.axis_index("head")
    plane, core = head // CORES, head % CORES
    for kind, ref in enumerate((queries, grads)):
        tokens = ref[...].astype(F32).reshape(TOKENS // 2, 2, PLANES, 8, HEAD_DIM)
        low, high = halves(tokens[:, 0], tokens[:, 1])
        mine = jnp.where(core == 0, low, high).astype(BF16)
        other = jnp.where(core == 0, high, low).astype(BF16)
        for target in range(PLANES):
            shift = (target - plane + PLANES) % PLANES
            keep[shift, kind] = mine[:, target].reshape(PIECE, HEAD_DIM)
            send[shift, kind] = other[:, target].reshape(PIECE, HEAD_DIM)


def split(rows, queries, grads):
    out = array(PLANES, 2, PIECE, HEAD_DIM)
    return pl.pallas_call(
        split_kernel,
        out_shape=(out, out),
        in_specs=[IN_SMEM, IN_VMEM, IN_VMEM],
        out_specs=(IN_VMEM, IN_VMEM),
        compiler_params=pltpu.CompilerParams(vmem_limit_bytes=VMEM_LIMIT),
        name="split_heads",
    )(rows, queries, grads)


def join_kernel(keep, got, *parcels):
    for shift, parcel in enumerate(parcels):
        parcel[0:2] = keep[shift]
        parcel[2:4] = got[shift]


def join(keep, got):
    return pl.pallas_call(
        join_kernel,
        out_shape=(array(4, PIECE, HEAD_DIM),) * PLANES,
        in_specs=[IN_VMEM, IN_VMEM],
        out_specs=(IN_VMEM,) * PLANES,
        compiler_params=pltpu.CompilerParams(vmem_limit_bytes=VMEM_LIMIT),
        name="join_parcels",
    )(keep, got)


def attend_kernel(slots, unused, fetched, *refs):
    parcels, terms, results = refs[:PLANES], refs[PLANES], refs[PLANES + 1 : 2 * PLANES + 1]
    q_rows, g_rows, key_rows, value_rows, grad_rows, score_buf, weight_buf, delta_buf, stage, sems = refs[2 * PLANES + 1 :]
    head = lax.axis_index("head")
    plane, core = head // CORES, head % CORES
    for shift, parcel in enumerate(parcels):
        source = (plane - shift + PLANES) % PLANES
        for piece, owner in ((0, core), (2, 1 - core)):
            span = pl.ds(pl.multiple_of((source * CORES + owner) * PIECE, 16), PIECE)
            q_rows[span, :] = parcel[piece]
            g_rows[span, :] = parcel[piece + 1]
    rows_last = (((1,), (1,)), ((), ()))
    rows_first = (((0,), (0,)), ((), ()))
    chunks = [pl.ds(start, CHUNK) for start in range(0, KEYS, CHUNK)]
    per_chunk = CHUNK // BLOCK

    def fold(values, reduce):
        return reduce(values.reshape(CHUNK // 8, 8, ROWS), axis=0)

    def store(step, s):
        item = step * SELECTED + s
        return pltpu.make_async_copy(stage.at[item], terms.at[slots[s, step]], sems.at[item])

    def block(step, carry):
        for s in range(SELECTED):
            slot = slots[s, step]
            key_rows[pl.ds(s * BLOCK, BLOCK), :] = fetched[slot, 0]
            value_rows[pl.ds(s * BLOCK, BLOCK), :] = fetched[slot, 1]
        span = pl.ds(pl.multiple_of(step * ROWS, ROWS), ROWS)
        q_now = q_rows[span, :]
        g_now = g_rows[span, :]
        peak = jnp.full((8, ROWS), -jnp.inf, F32)
        for chunk in chunks:
            scores = lax.dot_general(key_rows[chunk, :], q_now, rows_last, preferred_element_type=F32)
            score_buf[chunk, :] = scores
            peak = jnp.maximum(peak, fold(scores, jnp.max))
        peak = jnp.max(peak, axis=0, keepdims=True)
        total = jnp.zeros((8, ROWS), F32)
        delta = jnp.zeros((8, ROWS), F32)
        for chunk in chunks:
            weights = lax.dot_general(value_rows[chunk, :], g_now, rows_last, preferred_element_type=F32)
            lifted = jnp.exp2((score_buf[chunk, :] - peak) * (SCALE * LOG2E))
            score_buf[chunk, :] = lifted
            weight_buf[chunk, :] = weights
            total += fold(lifted, jnp.sum)
            delta += fold(lifted * weights, jnp.sum)
        inverse = 1.0 / jnp.sum(total, axis=0, keepdims=True)
        delta = jnp.sum(delta, axis=0, keepdims=True) * inverse
        for index, chunk in enumerate(chunks):
            attend = score_buf[chunk, :] * inverse
            score_grad = (attend * (weight_buf[chunk, :] - delta) * SCALE).astype(BF16)
            delta_buf[chunk, :] = score_grad
            key_terms = jnp.dot(score_grad, q_now, preferred_element_type=F32).astype(BF16)
            value_terms = jnp.dot(attend.astype(BF16), g_now, preferred_element_type=F32).astype(BF16)
            for part in range(per_chunk):
                s = index * per_chunk + part
                item = step * SELECTED + s
                stage[item, 0] = key_terms[part * BLOCK : (part + 1) * BLOCK]
                stage[item, 1] = value_terms[part * BLOCK : (part + 1) * BLOCK]
                store(step, s).start()
        query_terms = lax.dot_general(delta_buf[...], key_rows[...], rows_first, preferred_element_type=F32)
        grad_rows[span, :] = query_terms.astype(BF16)
        return carry

    lax.fori_loop(0, QBLOCKS, block, 0, unroll=True)
    for shift, result in enumerate(results):
        target = (plane + shift) % PLANES
        for owner in range(CORES):
            span = pl.ds(pl.multiple_of((target * CORES + owner) * PIECE, 16), PIECE)
            result[owner] = grad_rows[span, :]

    def finish(step, carry):
        for s in range(SELECTED):
            store(step, s).wait()
        return carry

    lax.fori_loop(0, QBLOCKS, finish, 0)


def attend_backward(slots, packed, fetched, parcels):
    rows = pltpu.VMEM((QBLOCKS * ROWS, HEAD_DIM), BF16)
    return pl.pallas_call(
        attend_kernel,
        out_shape=(array(CTX, 2, BLOCK, HEAD_DIM),) + (array(CORES, PIECE, HEAD_DIM),) * PLANES,
        in_specs=[IN_SMEM, IN_HBM, IN_VMEM] + [IN_VMEM] * PLANES,
        out_specs=(IN_HBM,) + (IN_VMEM,) * PLANES,
        scratch_shapes=[
            rows,
            rows,
            pltpu.VMEM((KEYS, HEAD_DIM), BF16),
            pltpu.VMEM((KEYS, HEAD_DIM), BF16),
            rows,
            pltpu.VMEM((KEYS, ROWS), F32),
            pltpu.VMEM((KEYS, ROWS), F32),
            pltpu.VMEM((KEYS, ROWS), BF16),
            pltpu.VMEM((QBLOCKS * SELECTED, 2, BLOCK, HEAD_DIM), BF16),
            pltpu.SemaphoreType.DMA((QBLOCKS * SELECTED,)),
        ],
        input_output_aliases={1: 0},
        compiler_params=pltpu.CompilerParams(vmem_limit_bytes=VMEM_ATTEND),
        name="attend_backward",
    )(slots, packed, fetched, *parcels)


def swap_kernel(*refs):
    parcels, (keep, send) = refs[:PLANES], refs[PLANES:]
    core = lax.axis_index("head") % CORES
    for shift, parcel in enumerate(parcels):
        keep[shift] = parcel[core]
        send[shift] = parcel[1 - core]


def swap(parcels):
    out = array(PLANES, PIECE, HEAD_DIM)
    return pl.pallas_call(
        swap_kernel,
        out_shape=(out, out),
        in_specs=[IN_VMEM] * PLANES,
        out_specs=(IN_VMEM, IN_VMEM),
        compiler_params=pltpu.CompilerParams(vmem_limit_bytes=VMEM_LIMIT),
        name="swap_cores",
    )(*parcels)


def merge_kernel(keep, got, query_grad):
    head = lax.axis_index("head")
    plane, core = head // CORES, head % CORES
    shape = (TOKENS // 2, 8, HEAD_DIM)
    even, odd = [], []
    for source in range(PLANES):
        shift = (plane - source + PLANES) % PLANES
        mine = keep[shift].astype(F32).reshape(shape)
        other = got[shift].astype(F32).reshape(shape)
        pair = halves(jnp.where(core == 0, mine, other), jnp.where(core == 0, other, mine))
        even.append(pair[0])
        odd.append(pair[1])
    both = jnp.stack([jnp.stack(even, 1), jnp.stack(odd, 1)], 1)
    query_grad[...] = both.reshape(TOKENS, PLANES * 8, HEAD_DIM).astype(BF16)


def merge(keep, got):
    return pl.pallas_call(
        merge_kernel,
        out_shape=array(TOKENS, PLANES * 8, HEAD_DIM),
        in_specs=[IN_VMEM, IN_VMEM],
        out_specs=IN_VMEM,
        compiler_params=pltpu.CompilerParams(vmem_limit_bytes=VMEM_LIMIT),
        name="merge_heads",
    )(keep, got)


def sum_kernel(rows, terms, key_grad, value_grad, sums, halves_out, sems):
    sums[...] = jnp.zeros_like(sums)

    def add(index, carry):
        row = wanted_row(rows, index)
        row = jnp.where(row < 0, OWNED, row)
        for kind in range(2):
            sums[kind, row] += terms[index, kind].astype(F32)
        return carry

    lax.fori_loop(0, CTX, add, 0, unroll=4)
    copies = []
    for kind, out in enumerate((key_grad, value_grad)):
        for part in range(2):
            span = pl.ds(part * (OWNED // 2), OWNED // 2)
            halves_out[kind, span] = sums[kind, span].astype(BF16)
            copies.append(pltpu.make_async_copy(halves_out.at[kind, span], out.at[span], sems.at[kind, part]))
            copies[-1].start()
    for copy in copies:
        copy.wait()


def owner_sum(rows, terms):
    grad = array(OWNED, BLOCK, HEAD_DIM)
    return pl.pallas_call(
        sum_kernel,
        out_shape=(grad, grad),
        in_specs=[IN_SMEM, IN_VMEM],
        out_specs=(IN_HBM, IN_HBM),
        scratch_shapes=[
            pltpu.VMEM((2, OWNED + 1, BLOCK, HEAD_DIM), F32),
            pltpu.VMEM((2, OWNED, BLOCK, HEAD_DIM), BF16),
            pltpu.SemaphoreType.DMA((2, 2)),
        ],
        compiler_params=pltpu.CompilerParams(vmem_limit_bytes=VMEM_LIMIT),
        name="owner_sum",
    )(rows, terms)


def exchange(blocks):
    return lax.all_to_all(blocks, "ctx", split_axis=0, concat_axis=0, tiled=True)


def swap_partner(array):
    return lax.ppermute(array, "head", [(i, i ^ 1) for i in range(PLANES * CORES)])


def along_planes(parcels):
    moved = [parcels[0]]
    for shift in range(1, PLANES):
        pairs = [(i, (i + shift * CORES) % (PLANES * CORES)) for i in range(PLANES * CORES)]
        moved.append(lax.ppermute(parcels[shift], "head", pairs))
    return moved


def per_device(queries, keys, values, out_grad, selected):
    ctx = lax.axis_index("ctx")
    table = selected[0].T
    slots = lax.dynamic_slice_in_dim(table, ctx * QBLOCKS, QBLOCKS, 1) // OWNED
    blocks = (OWNED, BLOCK, HEAD_DIM)
    packed, rows = pack(table, keys.reshape(blocks), values.reshape(blocks))
    fetched = exchange(packed)
    keep, send = split(rows, queries, out_grad)
    parcels = along_planes(join(keep, swap_partner(send)))
    terms, *results = attend_backward(slots, packed, fetched, parcels)
    back = exchange(terms)
    keep, send = swap(along_planes(results))
    query_grad = merge(keep, swap_partner(send))
    key_grad, value_grad = owner_sum(rows, back)
    return query_grad, key_grad.reshape(keys.shape), value_grad.reshape(values.shape)


def solution(mesh):
    tokens = P(("ctx", "head"), None, None)
    context = P("ctx", "head", None)
    return jax.shard_map(
        per_device,
        mesh=mesh,
        in_specs=(tokens, context, context, tokens, P("head", None, None)),
        out_specs=(tokens, context, context),
        check_vma=False,
    )
```

time: 148 us -> 144 us (0.973)
  the two profiles are of different devices: /device:TPU:666 before, /device:TPU:410 now
where the time goes in v3:
time: 144 us; the launch traced here: 143 us
  starting transfers between devices  93.1 us (65%)
  waiting for transfers between devices  36.6 us (25%)
  Pallas kernels  12.1 us (8%)
    ppermute x14, starting transfers between devices, along_planes(): moved.append(lax.ppermute(parcels[shift], 'head', pairs))  66.6 us
    all_to_all x2, waiting for transfers between devices, exchange(): lax.all_to_all(blocks, 'ctx', split_axis=0, concat_axis=0, tiled=True)  27.8 us
    all_to_all x2, starting transfers between devices, exchange(): lax.all_to_all(blocks, 'ctx', split_axis=0, concat_axis=0, tiled=True)  22.7 us
    ppermute x14, waiting for transfers between devices, along_planes(): moved.append(lax.ppermute(parcels[shift], 'head', pairs))  6.12 us
    pallas_call x1, Pallas kernels, attend_backward(): pl.pallas_call(attend_kernel, out_shape=(array(CTX, 2, BLOCK, HEAD_DIM),)...  5.03 us
    ppermute x2, starting transfers between devices, swap_partner(): lax.ppermute(array, 'head', [(i, i ^ 1) for i in range(PLANES * CORES)])  3.84 us
    pallas_call x1, Pallas kernels, pack(): pl.pallas_call(pack_kernel, out_shape=(array(CTX, 2, BLOCK, HEAD_DIM), ar...  3.35 us
  transfers between devices with their start and end apart: 18, of which 6 were waited for; matrix products, arithmetic and copies ran while one was open for 0% of the time, Pallas kernels for 1%

profile of v3, /device:TPU:410, one launch (start us, length us, event | category | flops | bytes accessed | tf_op | source)
XLA Modules:
  0.0 142.9 jit_solution(16507160956285245650)
XLA Ops:
  0.6 3.3 %pack_blocks.1 = (bf16[64,2,64,128]{3,2,1,0:T(8,128)(2,1)}, s32[1,192]{1,0:T(1,128)}) custom-call(s32[16,192]{1,0:T(8,128)} %bitcast.27, bf16[32,64,128]{2,1,0:T(8,128)(2,1)} %bitcast.25, bf16[32,64,128]{2,1,0:T(8,128)(2,1)} %bitcast.26), custom_call_target="tpu_custom_call" | custom-call | tf_op jit(solution)/shard_map/pack_blocks/pallas_call | solution.py:86
  4.0 0.0 copy-start
  4.0 0.0 copy-start.1
  4.0 0.0 copy-start.2
  4.0 0.0 copy-start.3
  4.0 13.5 %all-to-all-start = ((bf16[64,2,64,128]{3,2,1,0:T(8,128)(2,1)}), bf16[64,2,64,128]{3,2,1,0:T(8,128)(2,1)S(1)}, u32[]{:S(2)}, u32[]{:S(2)}) async-start(bf16[64,2,64,128]{3,2,1,0:T(8,128)(2,1)} %get-tuple-element.28.unused), calls=%async_computation | async-start | bytes 4194304 | tf_op jit(solution)/shard_map/all_to_all | solution.py:348
  17.6 0.0 copy-done
  17.6 0.7 split_heads.1
  18.3 1.9 %collective-permute-start = (bf16[8,2,48,128]{3,2,1,0:T(8,128)(2,1)S(1)}, bf16[8,2,48,128]{3,2,1,0:T(8,128)(2,1)S(1)}, u32[]{:S(2)}, u32[]{:S(2)}) collective-permute-start(bf16[8,2,48,128]{3,2,1,0:T(8,128)(2,1)S(1)} %get-tuple-element.31), channel_id=1, source_target_pairs={{0,1},{1,0},{2,3},{3,2},{4,5},{5,4},{6,7},{7,6},{8,9},{9,8},{10,11... | collective-permute-start | bytes 589832 | tf_op jit(solution)/shard_map/ppermute | solution.py:352
  20.2 1.4 collective-permute-done.got
  21.6 6.4 %collective-permute-start.1 = (bf16[4,48,128]{2,1,0:T(8,128)(2,1)S(1)}, bf16[4,48,128]{2,1,0:T(8,128)(2,1)S(1)}, u32[]{:S(2)}, u32[]{:S(2)}) collective-permute-start(bf16[4,48,128]{2,1,0:T(8,128)(2,1)S(1)} %get-tuple-element.33), channel_id=1, source_target_pairs={{0,2},{1,3},{2,4},{3,5},{4,6},{5,7},{6,8},{7,9},{8,10},{9,11},{10,... | collective-permute-start | bytes 147464 | tf_op jit(solution)/shard_map/ppermute | solution.py:359
  28.1 6.1 %collective-permute-start.2 = (bf16[4,48,128]{2,1,0:T(8,128)(2,1)S(1)}, bf16[4,48,128]{2,1,0:T(8,128)(2,1)S(1)}, u32[]{:S(2)}, u32[]{:S(2)}) collective-permute-start(bf16[4,48,128]{2,1,0:T(8,128)(2,1)S(1)} %get-tuple-element.34), channel_id=1, source_target_pairs={{0,4},{1,5},{2,6},{3,7},{4,8},{5,9},{6,10},{7,11},{8,12},{9,13},{1... | collective-permute-start | bytes 147464 | tf_op jit(solution)/shard_map/ppermute | solution.py:359
  34.2 3.7 %collective-permute-start.3 = (bf16[4,48,128]{2,1,0:T(8,128)(2,1)S(1)}, bf16[4,48,128]{2,1,0:T(8,128)(2,1)S(1)}, u32[]{:S(2)}, u32[]{:S(2)}) collective-permute-start(bf16[4,48,128]{2,1,0:T(8,128)(2,1)S(1)} %get-tuple-element.35), channel_id=1, source_target_pairs={{0,6},{1,7},{2,8},{3,9},{4,10},{5,11},{6,12},{7,13},{8,14},{9,15},... | collective-permute-start | bytes 147464 | tf_op jit(solution)/shard_map/ppermute | solution.py:359
  37.9 4.2 %collective-permute-start.4 = (bf16[4,48,128]{2,1,0:T(8,128)(2,1)S(1)}, bf16[4,48,128]{2,1,0:T(8,128)(2,1)S(1)}, u32[]{:S(2)}, u32[]{:S(2)}) collective-permute-start(bf16[4,48,128]{2,1,0:T(8,128)(2,1)S(1)} %get-tuple-element.36), channel_id=1, source_target_pairs={{0,8},{1,9},{2,10},{3,11},{4,12},{5,13},{6,14},{7,15},{8,0},{9,1},... | collective-permute-start | bytes 147464 | tf_op jit(solution)/shard_map/ppermute | solution.py:359
  42.1 3.4 %collective-permute-start.5 = (bf16[4,48,128]{2,1,0:T(8,128)(2,1)S(1)}, bf16[4,48,128]{2,1,0:T(8,128)(2,1)S(1)}, u32[]{:S(2)}, u32[]{:S(2)}) collective-permute-start(bf16[4,48,128]{2,1,0:T(8,128)(2,1)S(1)} %get-tuple-element.37), channel_id=1, source_target_pairs={{0,10},{1,11},{2,12},{3,13},{4,14},{5,15},{6,0},{7,1},{8,2},{9,3},... | collective-permute-start | bytes 147464 | tf_op jit(solution)/shard_map/ppermute | solution.py:359
  45.6 0.0 collective-permute-done.1.refs_1_
  45.6 5.5 %collective-permute-start.6 = (bf16[4,48,128]{2,1,0:T(8,128)(2,1)S(1)}, bf16[4,48,128]{2,1,0:T(8,128)(2,1)S(1)}, u32[]{:S(2)}, u32[]{:S(2)}) collective-permute-start(bf16[4,48,128]{2,1,0:T(8,128)(2,1)S(1)} %get-tuple-element.38), channel_id=1, source_target_pairs={{0,12},{1,13},{2,14},{3,15},{4,0},{5,1},{6,2},{7,3},{8,4},{9,5},{1... | collective-permute-start | bytes 147464 | tf_op jit(solution)/shard_map/ppermute | solution.py:359
  51.1 0.0 collective-permute-done.2.refs_2_
  51.1 3.9 %collective-permute-start.7 = (bf16[4,48,128]{2,1,0:T(8,128)(2,1)S(1)}, bf16[4,48,128]{2,1,0:T(8,128)(2,1)S(1)}, u32[]{:S(2)}, u32[]{:S(2)}) collective-permute-start(bf16[4,48,128]{2,1,0:T(8,128)(2,1)S(1)} %get-tuple-element.39), channel_id=1, source_target_pairs={{0,14},{1,15},{2,0},{3,1},{4,2},{5,3},{6,4},{7,5},{8,6},{9,7},{10,... | collective-permute-start | bytes 147464 | tf_op jit(solution)/shard_map/ppermute | solution.py:359
  55.0 0.0 copy-done.3
  55.0 0.1 add_select_fusion.slots
  55.1 0.0 collective-permute-done.3.refs_3_
  55.1 0.0 collective-permute-done.4.refs_4_
  55.1 0.0 collective-permute-done.5.refs_5_
  55.1 0.0 collective-permute-done.6.refs_6_
  55.2 3.1 %collective-permute-done.7.refs_7_ = bf16[4,48,128]{2,1,0:T(8,128)(2,1)S(1)} collective-permute-done((bf16[4,48,128]{2,1,0:T(8,128)(2,1)S(1)}, bf16[4,48,128]{2,1,0:T(8,128)(2,1)S(1)}, u32[]{:S(2)}, u32[]{:S(2)}) %collective-permute-start.7) | collective-permute-done | bytes 49184 | tf_op jit(solution)/shard_map/ppermute | solution.py:359
  58.3 13.3 %all-to-all-done.fetched = bf16[64,2,64,128]{3,2,1,0:T(8,128)(2,1)S(1)} async-done(((bf16[64,2,64,128]{3,2,1,0:T(8,128)(2,1)}), bf16[64,2,64,128]{3,2,1,0:T(8,128)(2,1)S(1)}, u32[]{:S(2)}, u32[]{:S(2)}) %all-to-all-start) | async-done | bytes 2097184 | tf_op jit(solution)/shard_map/all_to_all | solution.py:348
  71.6 5.0 %attend_backward.1 = (bf16[64,2,64,128]{3,2,1,0:T(8,128)(2,1)}, bf16[2,48,128]{2,1,0:T(8,128)(2,1)S(1)}, bf16[2,48,128]{2,1,0:T(8,128)(2,1)S(1)}, bf16[2,48,128]...) custom-call(s32[16,3]{1,0:T(8,128)S(1)} %add_select_fusion.slots, ...), custom_call_target="tpu_custom_call", output_to_operand_aliasing={{0}: (1, {})} | custom-call | tf_op jit(solution)/shard_map/attend_backward/pallas_call | solution.py:238
  76.7 9.2 %all-to-all-start.1 = ((bf16[64,2,64,128]{3,2,1,0:T(8,128)(2,1)}), bf16[64,2,64,128]{3,2,1,0:T(8,128)(2,1)S(1)}, u32[]{:S(2)}, u32[]{:S(2)}) async-start(bf16[64,2,64,128]{3,2,1,0:T(8,128)(2,1)} %get-tuple-element.50), calls=%async_computation.1 | async-start | bytes 4194304 | tf_op jit(solution)/shard_map/all_to_all | solution.py:348
  85.8 6.4 %collective-permute-start.8 = (bf16[2,48,128]{2,1,0:T(8,128)(2,1)S(1)}, bf16[2,48,128]{2,1,0:T(8,128)(2,1)S(1)}, u32[]{:S(2)}, u32[]{:S(2)}) collective-permute-start(bf16[2,48,128]{2,1,0:T(8,128)(2,1)S(1)} %get-tuple-element.41), channel_id=1, source_target_pairs={{0,2},{1,3},{2,4},{3,5},{4,6},{5,7},{6,8},{7,9},{8,10},{9,11},{10,... | collective-permute-start | bytes 73736 | tf_op jit(solution)/shard_map/ppermute | solution.py:359
  92.2 6.1 %collective-permute-start.9 = (bf16[2,48,128]{2,1,0:T(8,128)(2,1)S(1)}, bf16[2,48,128]{2,1,0:T(8,128)(2,1)S(1)}, u32[]{:S(2)}, u32[]{:S(2)}) collective-permute-start(bf16[2,48,128]{2,1,0:T(8,128)(2,1)S(1)} %get-tuple-element.42), channel_id=1, source_target_pairs={{0,4},{1,5},{2,6},{3,7},{4,8},{5,9},{6,10},{7,11},{8,12},{9,13},{1... | collective-permute-start | bytes 73736 | tf_op jit(solution)/shard_map/ppermute | solution.py:359
  98.4 3.7 %collective-permute-start.10 = (bf16[2,48,128]{2,1,0:T(8,128)(2,1)S(1)}, bf16[2,48,128]{2,1,0:T(8,128)(2,1)S(1)}, u32[]{:S(2)}, u32[]{:S(2)}) collective-permute-start(bf16[2,48,128]{2,1,0:T(8,128)(2,1)S(1)} %get-tuple-element.43), channel_id=1, source_target_pairs={{0,6},{1,7},{2,8},{3,9},{4,10},{5,11},{6,12},{7,13},{8,14},{9,15},... | collective-permute-start | bytes 73736 | tf_op jit(solution)/shard_map/ppermute | solution.py:359
  102.1 4.2 %collective-permute-start.11 = (bf16[2,48,128]{2,1,0:T(8,128)(2,1)S(1)}, bf16[2,48,128]{2,1,0:T(8,128)(2,1)S(1)}, u32[]{:S(2)}, u32[]{:S(2)}) collective-permute-start(bf16[2,48,128]{2,1,0:T(8,128)(2,1)S(1)} %get-tuple-element.44), channel_id=1, source_target_pairs={{0,8},{1,9},{2,10},{3,11},{4,12},{5,13},{6,14},{7,15},{8,0},{9,1},... | collective-permute-start | bytes 73736 | tf_op jit(solution)/shard_map/ppermute | solution.py:359
  106.3 3.4 %collective-permute-start.12 = (bf16[2,48,128]{2,1,0:T(8,128)(2,1)S(1)}, bf16[2,48,128]{2,1,0:T(8,128)(2,1)S(1)}, u32[]{:S(2)}, u32[]{:S(2)}) collective-permute-start(bf16[2,48,128]{2,1,0:T(8,128)(2,1)S(1)} %get-tuple-element.45), channel_id=1, source_target_pairs={{0,10},{1,11},{2,12},{3,13},{4,14},{5,15},{6,0},{7,1},{8,2},{9,3},... | collective-permute-start | bytes 73736 | tf_op jit(solution)/shard_map/ppermute | solution.py:359
  109.8 0.0 collective-permute-done.8.refs_1_
  109.8 5.5 %collective-permute-start.13 = (bf16[2,48,128]{2,1,0:T(8,128)(2,1)S(1)}, bf16[2,48,128]{2,1,0:T(8,128)(2,1)S(1)}, u32[]{:S(2)}, u32[]{:S(2)}) collective-permute-start(bf16[2,48,128]{2,1,0:T(8,128)(2,1)S(1)} %get-tuple-element.46), channel_id=1, source_target_pairs={{0,12},{1,13},{2,14},{3,15},{4,0},{5,1},{6,2},{7,3},{8,4},{9,5},{1... | collective-permute-start | bytes 73736 | tf_op jit(solution)/shard_map/ppermute | solution.py:359
  115.3 0.0 collective-permute-done.9.refs_2_
  115.3 3.9 %collective-permute-start.14 = (bf16[2,48,128]{2,1,0:T(8,128)(2,1)S(1)}, bf16[2,48,128]{2,1,0:T(8,128)(2,1)S(1)}, u32[]{:S(2)}, u32[]{:S(2)}) collective-permute-start(bf16[2,48,128]{2,1,0:T(8,128)(2,1)S(1)} %get-tuple-element.47), channel_id=1, source_target_pairs={{0,14},{1,15},{2,0},{3,1},{4,2},{5,3},{6,4},{7,5},{8,6},{9,7},{10,... | collective-permute-start | bytes 73736 | tf_op jit(solution)/shard_map/ppermute | solution.py:359
  119.2 0.0 collective-permute-done.10.refs_3_
  119.2 0.0 collective-permute-done.11.refs_4_
  119.2 0.0 collective-permute-done.12.refs_5_
  119.2 0.0 collective-permute-done.13.refs_6_
  119.2 3.0 %collective-permute-done.14.refs_7_ = bf16[2,48,128]{2,1,0:T(8,128)(2,1)S(1)} collective-permute-done((bf16[2,48,128]{2,1,0:T(8,128)(2,1)S(1)}, bf16[2,48,128]{2,1,0:T(8,128)(2,1)S(1)}, u32[]{:S(2)}, u32[]{:S(2)}) %collective-permute-start.14) | collective-permute-done | bytes 24608 | tf_op jit(solution)/shard_map/ppermute | solution.py:359
  122.2 1.9 %collective-permute-start.15 = (bf16[8,48,128]{2,1,0:T(8,128)(2,1)S(1)}, bf16[8,48,128]{2,1,0:T(8,128)(2,1)S(1)}, u32[]{:S(2)}, u32[]{:S(2)}) collective-permute-start(bf16[8,48,128]{2,1,0:T(8,128)(2,1)S(1)} %get-tuple-element.49), channel_id=1, source_target_pairs={{0,1},{1,0},{2,3},{3,2},{4,5},{5,4},{6,7},{7,6},{8,9},{9,8},{10,11... | collective-permute-start | bytes 294920 | tf_op jit(solution)/shard_map/ppermute | solution.py:352
  124.1 1.3 collective-permute-done.15.got
  125.4 0.7 merge_heads.1
  126.2 14.4 %all-to-all-done.1.terms = bf16[64,2,64,128]{3,2,1,0:T(8,128)(2,1)S(1)} async-done(((bf16[64,2,64,128]{3,2,1,0:T(8,128)(2,1)}), bf16[64,2,64,128]{3,2,1,0:T(8,128)(2,1)S(1)}, u32[]{:S(2)}, u32[]{:S(2)}) %all-to-all-start.1) | async-done | bytes 2097184 | tf_op jit(solution)/shard_map/all_to_all | solution.py:348
  140.6 2.3 %owner_sum.1 = (bf16[32,64,128]{2,1,0:T(8,128)(2,1)}, bf16[32,64,128]{2,1,0:T(8,128)(2,1)}) custom-call(s32[1,192]{1,0:T(1,128)S(1)} %copy-done.2, bf16[64,2,64,128]{3,2,1,0:T(8,128)(2,1)S(1)} %all-to-all-done.1.terms), custom_call_target="tpu_custom_call" | custom-call | tf_op jit(solution)/shard_map/owner_sum/pallas_call | solution.py:332
  (4 shorter events, 0.0 us)
Async XLA Ops:
  4.0 13.6 %copy-start = (bf16[12,64,128]{2,1,0:T(8,128)(2,1)S(1)}, bf16[12,64,128]{2,1,0:T(8,128)(2,1)}, u32[]{:S(2)}) copy-start(bf16[12,64,128]{2,1,0:T(8,128)(2,1)} %queries.1) | copy-start | bytes 589828
  4.0 13.6 %copy-start.1 = (bf16[12,64,128]{2,1,0:T(8,128)(2,1)S(1)}, bf16[12,64,128]{2,1,0:T(8,128)(2,1)}, u32[]{:S(2)}) copy-start(bf16[12,64,128]{2,1,0:T(8,128)(2,1)} %grads.1) | copy-start | bytes 589828
  4.0 13.6 %copy-start.2 = (s32[1,192]{1,0:T(1,128)S(1)}, s32[1,192]{1,0:T(1,128)}, u32[]{:S(2)}) copy-start(s32[1,192]{1,0:T(1,128)} %get-tuple-element.29.rows) | copy-start | bytes 2308
  4.0 51.0 %copy-start.3 = (s32[1,192,16]{1,2,0:T(8,128)S(1)}, s32[1,192,16]{1,2,0:T(8,128)}, u32[]{:S(2)}) copy-start(s32[1,192,16]{1,2,0:T(8,128)} %param.9) | copy-start | bytes 36868
  4.0 67.6 %all-to-all-start = ((bf16[64,2,64,128]{3,2,1,0:T(8,128)(2,1)}), bf16[64,2,64,128]{3,2,1,0:T(8,128)(2,1)S(1)}, u32[]{:S(2)}, u32[]{:S(2)}) async-start(bf16[64,2,64,128]{3,2,1,0:T(8,128)(2,1)} %get-tuple-element.28.unused), calls=%async_computation | async-start | bytes 4194304 | tf_op jit(solution)/shard_map/all_to_all | solution.py:348
  18.3 3.3 %collective-permute-start = (bf16[8,2,48,128]{3,2,1,0:T(8,128)(2,1)S(1)}, bf16[8,2,48,128]{3,2,1,0:T(8,128)(2,1)S(1)}, u32[]{:S(2)}, u32[]{:S(2)}) collective-permute-start(bf16[8,2,48,128]{3,2,1,0:T(8,128)(2,1)S(1)} %get-tuple-element.31), channel_id=1, source_target_pairs={{0,1},{1,0},{2,3},{3,2},{4,5},{5,4},{6,7},{7,6},{8,9},{9,8},{10,11... | collective-permute-start | bytes 589832 | tf_op jit(solution)/shard_map/ppermute | solution.py:352
  21.6 23.9 %collective-permute-start.1 = (bf16[4,48,128]{2,1,0:T(8,128)(2,1)S(1)}, bf16[4,48,128]{2,1,0:T(8,128)(2,1)S(1)}, u32[]{:S(2)}, u32[]{:S(2)}) collective-permute-start(bf16[4,48,128]{2,1,0:T(8,128)(2,1)S(1)} %get-tuple-element.33), channel_id=1, source_target_pairs={{0,2},{1,3},{2,4},{3,5},{4,6},{5,7},{6,8},{7,9},{8,10},{9,11},{10,... | collective-permute-start | bytes 147464 | tf_op jit(solution)/shard_map/ppermute | solution.py:359
  28.1 23.0 %collective-permute-start.2 = (bf16[4,48,128]{2,1,0:T(8,128)(2,1)S(1)}, bf16[4,48,128]{2,1,0:T(8,128)(2,1)S(1)}, u32[]{:S(2)}, u32[]{:S(2)}) collective-permute-start(bf16[4,48,128]{2,1,0:T(8,128)(2,1)S(1)} %get-tuple-element.34), channel_id=1, source_target_pairs={{0,4},{1,5},{2,6},{3,7},{4,8},{5,9},{6,10},{7,11},{8,12},{9,13},{1... | collective-permute-start | bytes 147464 | tf_op jit(solution)/shard_map/ppermute | solution.py:359
  34.2 20.9 %collective-permute-start.3 = (bf16[4,48,128]{2,1,0:T(8,128)(2,1)S(1)}, bf16[4,48,128]{2,1,0:T(8,128)(2,1)S(1)}, u32[]{:S(2)}, u32[]{:S(2)}) collective-permute-start(bf16[4,48,128]{2,1,0:T(8,128)(2,1)S(1)} %get-tuple-element.35), channel_id=1, source_target_pairs={{0,6},{1,7},{2,8},{3,9},{4,10},{5,11},{6,12},{7,13},{8,14},{9,15},... | collective-permute-start | bytes 147464 | tf_op jit(solution)/shard_map/ppermute | solution.py:359
  37.9 17.2 %collective-permute-start.4 = (bf16[4,48,128]{2,1,0:T(8,128)(2,1)S(1)}, bf16[4,48,128]{2,1,0:T(8,128)(2,1)S(1)}, u32[]{:S(2)}, u32[]{:S(2)}) collective-permute-start(bf16[4,48,128]{2,1,0:T(8,128)(2,1)S(1)} %get-tuple-element.36), channel_id=1, source_target_pairs={{0,8},{1,9},{2,10},{3,11},{4,12},{5,13},{6,14},{7,15},{8,0},{9,1},... | collective-permute-start | bytes 147464 | tf_op jit(solution)/shard_map/ppermute | solution.py:359
  42.1 13.0 %collective-permute-start.5 = (bf16[4,48,128]{2,1,0:T(8,128)(2,1)S(1)}, bf16[4,48,128]{2,1,0:T(8,128)(2,1)S(1)}, u32[]{:S(2)}, u32[]{:S(2)}) collective-permute-start(bf16[4,48,128]{2,1,0:T(8,128)(2,1)S(1)} %get-tuple-element.37), channel_id=1, source_target_pairs={{0,10},{1,11},{2,12},{3,13},{4,14},{5,15},{6,0},{7,1},{8,2},{9,3},... | collective-permute-start | bytes 147464 | tf_op jit(solution)/shard_map/ppermute | solution.py:359
  45.6 9.6 %collective-permute-start.6 = (bf16[4,48,128]{2,1,0:T(8,128)(2,1)S(1)}, bf16[4,48,128]{2,1,0:T(8,128)(2,1)S(1)}, u32[]{:S(2)}, u32[]{:S(2)}) collective-permute-start(bf16[4,48,128]{2,1,0:T(8,128)(2,1)S(1)} %get-tuple-element.38), channel_id=1, source_target_pairs={{0,12},{1,13},{2,14},{3,15},{4,0},{5,1},{6,2},{7,3},{8,4},{9,5},{1... | collective-permute-start | bytes 147464 | tf_op jit(solution)/shard_map/ppermute | solution.py:359
  51.1 7.2 %collective-permute-start.7 = (bf16[4,48,128]{2,1,0:T(8,128)(2,1)S(1)}, bf16[4,48,128]{2,1,0:T(8,128)(2,1)S(1)}, u32[]{:S(2)}, u32[]{:S(2)}) collective-permute-start(bf16[4,48,128]{2,1,0:T(8,128)(2,1)S(1)} %get-tuple-element.39), channel_id=1, source_target_pairs={{0,14},{1,15},{2,0},{3,1},{4,2},{5,3},{6,4},{7,5},{8,6},{9,7},{10,... | collective-permute-start | bytes 147464 | tf_op jit(solution)/shard_map/ppermute | solution.py:359
  76.7 63.9 %all-to-all-start.1 = ((bf16[64,2,64,128]{3,2,1,0:T(8,128)(2,1)}), bf16[64,2,64,128]{3,2,1,0:T(8,128)(2,1)S(1)}, u32[]{:S(2)}, u32[]{:S(2)}) async-start(bf16[64,2,64,128]{3,2,1,0:T(8,128)(2,1)} %get-tuple-element.50), calls=%async_computation.1 | async-start | bytes 4194304 | tf_op jit(solution)/shard_map/all_to_all | solution.py:348
  85.8 23.9 %collective-permute-start.8 = (bf16[2,48,128]{2,1,0:T(8,128)(2,1)S(1)}, bf16[2,48,128]{2,1,0:T(8,128)(2,1)S(1)}, u32[]{:S(2)}, u32[]{:S(2)}) collective-permute-start(bf16[2,48,128]{2,1,0:T(8,128)(2,1)S(1)} %get-tuple-element.41), channel_id=1, source_target_pairs={{0,2},{1,3},{2,4},{3,5},{4,6},{5,7},{6,8},{7,9},{8,10},{9,11},{10,... | collective-permute-start | bytes 73736 | tf_op jit(solution)/shard_map/ppermute | solution.py:359
  92.2 23.0 %collective-permute-start.9 = (bf16[2,48,128]{2,1,0:T(8,128)(2,1)S(1)}, bf16[2,48,128]{2,1,0:T(8,128)(2,1)S(1)}, u32[]{:S(2)}, u32[]{:S(2)}) collective-permute-start(bf16[2,48,128]{2,1,0:T(8,128)(2,1)S(1)} %get-tuple-element.42), channel_id=1, source_target_pairs={{0,4},{1,5},{2,6},{3,7},{4,8},{5,9},{6,10},{7,11},{8,12},{9,13},{1... | collective-permute-start | bytes 73736 | tf_op jit(solution)/shard_map/ppermute | solution.py:359
  98.4 20.8 %collective-permute-start.10 = (bf16[2,48,128]{2,1,0:T(8,128)(2,1)S(1)}, bf16[2,48,128]{2,1,0:T(8,128)(2,1)S(1)}, u32[]{:S(2)}, u32[]{:S(2)}) collective-permute-start(bf16[2,48,128]{2,1,0:T(8,128)(2,1)S(1)} %get-tuple-element.43), channel_id=1, source_target_pairs={{0,6},{1,7},{2,8},{3,9},{4,10},{5,11},{6,12},{7,13},{8,14},{9,15},... | collective-permute-start | bytes 73736 | tf_op jit(solution)/shard_map/ppermute | solution.py:359
  102.1 17.1 %collective-permute-start.11 = (bf16[2,48,128]{2,1,0:T(8,128)(2,1)S(1)}, bf16[2,48,128]{2,1,0:T(8,128)(2,1)S(1)}, u32[]{:S(2)}, u32[]{:S(2)}) collective-permute-start(bf16[2,48,128]{2,1,0:T(8,128)(2,1)S(1)} %get-tuple-element.44), channel_id=1, source_target_pairs={{0,8},{1,9},{2,10},{3,11},{4,12},{5,13},{6,14},{7,15},{8,0},{9,1},... | collective-permute-start | bytes 73736 | tf_op jit(solution)/shard_map/ppermute | solution.py:359
  106.3 12.9 %collective-permute-start.12 = (bf16[2,48,128]{2,1,0:T(8,128)(2,1)S(1)}, bf16[2,48,128]{2,1,0:T(8,128)(2,1)S(1)}, u32[]{:S(2)}, u32[]{:S(2)}) collective-permute-start(bf16[2,48,128]{2,1,0:T(8,128)(2,1)S(1)} %get-tuple-element.45), channel_id=1, source_target_pairs={{0,10},{1,11},{2,12},{3,13},{4,14},{5,15},{6,0},{7,1},{8,2},{9,3},... | collective-permute-start | bytes 73736 | tf_op jit(solution)/shard_map/ppermute | solution.py:359
  109.8 9.5 %collective-permute-start.13 = (bf16[2,48,128]{2,1,0:T(8,128)(2,1)S(1)}, bf16[2,48,128]{2,1,0:T(8,128)(2,1)S(1)}, u32[]{:S(2)}, u32[]{:S(2)}) collective-permute-start(bf16[2,48,128]{2,1,0:T(8,128)(2,1)S(1)} %get-tuple-element.46), channel_id=1, source_target_pairs={{0,12},{1,13},{2,14},{3,15},{4,0},{5,1},{6,2},{7,3},{8,4},{9,5},{1... | collective-permute-start | bytes 73736 | tf_op jit(solution)/shard_map/ppermute | solution.py:359
  115.3 6.9 %collective-permute-start.14 = (bf16[2,48,128]{2,1,0:T(8,128)(2,1)S(1)}, bf16[2,48,128]{2,1,0:T(8,128)(2,1)S(1)}, u32[]{:S(2)}, u32[]{:S(2)}) collective-permute-start(bf16[2,48,128]{2,1,0:T(8,128)(2,1)S(1)} %get-tuple-element.47), channel_id=1, source_target_pairs={{0,14},{1,15},{2,0},{3,1},{4,2},{5,3},{6,4},{7,5},{8,6},{9,7},{10,... | collective-permute-start | bytes 73736 | tf_op jit(solution)/shard_map/ppermute | solution.py:359
  122.2 3.2 %collective-permute-start.15 = (bf16[8,48,128]{2,1,0:T(8,128)(2,1)S(1)}, bf16[8,48,128]{2,1,0:T(8,128)(2,1)S(1)}, u32[]{:S(2)}, u32[]{:S(2)}) collective-permute-start(bf16[8,48,128]{2,1,0:T(8,128)(2,1)S(1)} %get-tuple-element.49), channel_id=1, source_target_pairs={{0,1},{1,0},{2,3},{3,2},{4,5},{5,4},{6,7},{7,6},{8,9},{9,8},{10,11... | collective-permute-start | bytes 294920 | tf_op jit(solution)/shard_map/ppermute | solution.py:352

commit v4 on v3

--- a/solution.py
+++ b/solution.py
@@ -1,5 +1,3 @@
-import functools
-
 import jax
 import jax.numpy as jnp
 from jax import lax
@@ -20,7 +18,8 @@
 TOKENS = 12
 PIECE = TOKENS * GROUP_HEADS
 PLANES = 8
-CHUNK = 256
+PAIRS = 4
+CHUNK = 512
 CORES = 2
 SCALE = HEAD_DIM**-0.5
 LOG2E = 1.4426950408889634
@@ -102,6 +101,15 @@
     )(table, keys, values)
 
 
+def position():
+    head = lax.axis_index("head")
+    return head // (2 * CORES), head // CORES % 2, head % CORES
+
+
+def plane_at(pair, low):
+    return (pair + 2 * PAIRS) % PAIRS * 2 + low % 2
+
+
 def halves(first, second):
     low = lax.broadcasted_iota(jnp.int32, first.shape, first.ndim - 2) < GROUP_HEADS
     axis = first.ndim - 2
@@ -112,15 +120,14 @@
 
 
 def split_kernel(rows, queries, grads, keep, send):
-    head = lax.axis_index("head")
-    plane, core = head // CORES, head % CORES
+    pair, low_bit, core = position()
     for kind, ref in enumerate((queries, grads)):
         tokens = ref[...].astype(F32).reshape(TOKENS // 2, 2, PLANES, 8, HEAD_DIM)
         low, high = halves(tokens[:, 0], tokens[:, 1])
         mine = jnp.where(core == 0, low, high).astype(BF16)
         other = jnp.where(core == 0, high, low).astype(BF16)
         for target in range(PLANES):
-            shift = (target - plane + PLANES) % PLANES
+            shift = (target % 2 + low_bit) % 2 * PAIRS + (target // 2 - pair + PAIRS) % PAIRS
             keep[shift, kind] = mine[:, target].reshape(PIECE, HEAD_DIM)
             send[shift, kind] = other[:, target].reshape(PIECE, HEAD_DIM)
 
@@ -137,35 +144,68 @@
     )(rows, queries, grads)
 
 
-def join_kernel(keep, got, *parcels):
+def join_kernel(keep, got, near, far):
+    for shift in range(PAIRS):
+        near[shift, 0:2] = keep[shift]
+        near[shift, 2:4] = got[shift]
+        far[shift, 0:2] = keep[PAIRS + shift]
+        far[shift, 2:4] = got[PAIRS + shift]
+
+
+def link_kernel(near, far, *parcels):
     for shift, parcel in enumerate(parcels):
-        parcel[0:2] = keep[shift]
-        parcel[2:4] = got[shift]
-
-
-def join(keep, got):
-    return pl.pallas_call(
-        join_kernel,
-        out_shape=(array(4, PIECE, HEAD_DIM),) * PLANES,
-        in_specs=[IN_VMEM, IN_VMEM],
-        out_specs=(IN_VMEM,) * PLANES,
+        parcel[0] = near[shift]
+        parcel[1] = far[shift]
+
+
+def part_kernel(*refs):
+    parcels, (near, far) = refs[:PAIRS], refs[PAIRS:]
+    for shift, parcel in enumerate(parcels):
+        near[shift] = parcel[0]
+        far[shift] = parcel[1]
+
+
+def local(kernel, out_shape, name, *operands):
+    return pl.pallas_call(
+        kernel,
+        out_shape=out_shape,
+        in_specs=[IN_VMEM] * len(operands),
+        out_specs=(IN_VMEM,) * len(out_shape),
         compiler_params=pltpu.CompilerParams(vmem_limit_bytes=VMEM_LIMIT),
-        name="join_parcels",
-    )(keep, got)
-
-
-def attend_kernel(slots, unused, fetched, *refs):
-    parcels, terms, results = refs[:PLANES], refs[PLANES], refs[PLANES + 1 : 2 * PLANES + 1]
-    q_rows, g_rows, key_rows, value_rows, grad_rows, score_buf, weight_buf, delta_buf, stage, sems = refs[2 * PLANES + 1 :]
-    head = lax.axis_index("head")
-    plane, core = head // CORES, head % CORES
+        name=name,
+    )(*operands)
+
+
+def assemble_kernel(*refs):
+    parcels, (q_rows, g_rows) = refs[:PAIRS], refs[PAIRS:]
+    pair, low_bit, core = position()
     for shift, parcel in enumerate(parcels):
-        source = (plane - shift + PLANES) % PLANES
-        for piece, owner in ((0, core), (2, 1 - core)):
-            span = pl.ds(pl.multiple_of((source * CORES + owner) * PIECE, 16), PIECE)
-            q_rows[span, :] = parcel[piece]
-            g_rows[span, :] = parcel[piece + 1]
-    rows_last = (((1,), (1,)), ((), ()))
+        for other in range(2):
+            source = plane_at(pair - shift, low_bit + other)
+            for piece, owner in ((0, core), (2, 1 - core)):
+                span = pl.ds(pl.multiple_of((source * CORES + owner) * PIECE, 16), PIECE)
+                q_rows[span, :] = parcel[other, piece]
+                g_rows[span, :] = parcel[other, piece + 1]
+
+
+def assemble(parcels):
+    rows = array(QBLOCKS * ROWS, HEAD_DIM)
+    return local(assemble_kernel, (rows, rows), "assemble_rows", *parcels)
+
+
+def spread(grad_rows, results):
+    pair, low_bit, core = position()
+    for shift, result in enumerate(results):
+        for other in range(2):
+            target = plane_at(pair + shift, low_bit + other)
+            for owner in range(CORES):
+                span = pl.ds(pl.multiple_of((target * CORES + owner) * PIECE, 16), PIECE)
+                result[other, owner] = grad_rows[span, :]
+
+
+def attend_kernel(slots, unused, fetched, q_rows, g_rows, *refs):
+    terms, results = refs[0], refs[1 : PAIRS + 1]
+    all_keys, all_values, grad_rows, all_scores, all_weights, all_deltas, stage, sems = refs[PAIRS + 1 :]
     rows_first = (((0,), (0,)), ((), ()))
     chunks = [pl.ds(start, CHUNK) for start in range(0, KEYS, CHUNK)]
     per_chunk = CHUNK // BLOCK
@@ -177,24 +217,31 @@
         item = step * SELECTED + s
         return pltpu.make_async_copy(stage.at[item], terms.at[slots[s, step]], sems.at[item])
 
-    def block(step, carry):
+    def first(step):
+        key_rows, value_rows = all_keys.at[step], all_values.at[step]
+        score_buf, weight_buf, delta_buf = all_scores.at[step], all_weights.at[step], all_deltas.at[step]
         for s in range(SELECTED):
             slot = slots[s, step]
             key_rows[pl.ds(s * BLOCK, BLOCK), :] = fetched[slot, 0]
             value_rows[pl.ds(s * BLOCK, BLOCK), :] = fetched[slot, 1]
-        span = pl.ds(pl.multiple_of(step * ROWS, ROWS), ROWS)
+        span = pl.ds(step * ROWS, ROWS)
         q_now = q_rows[span, :]
         g_now = g_rows[span, :]
+        q_flip, g_flip = q_now.T, g_now.T
         peak = jnp.full((8, ROWS), -jnp.inf, F32)
         for chunk in chunks:
-            scores = lax.dot_general(key_rows[chunk, :], q_now, rows_last, preferred_element_type=F32)
+            scores = jnp.dot(key_rows[chunk, :], q_flip, preferred_element_type=F32)
             score_buf[chunk, :] = scores
             peak = jnp.maximum(peak, fold(scores, jnp.max))
         peak = jnp.max(peak, axis=0, keepdims=True)
+        return key_rows, value_rows, score_buf, weight_buf, delta_buf, span, q_now, g_now, g_flip, peak
+
+    def second(step, state):
+        key_rows, value_rows, score_buf, weight_buf, delta_buf, span, q_now, g_now, g_flip, peak = state
         total = jnp.zeros((8, ROWS), F32)
         delta = jnp.zeros((8, ROWS), F32)
         for chunk in chunks:
-            weights = lax.dot_general(value_rows[chunk, :], g_now, rows_last, preferred_element_type=F32)
+            weights = jnp.dot(value_rows[chunk, :], g_flip, preferred_element_type=F32)
             lifted = jnp.exp2((score_buf[chunk, :] - peak) * (SCALE * LOG2E))
             score_buf[chunk, :] = lifted
             weight_buf[chunk, :] = weights
@@ -216,14 +263,13 @@
                 store(step, s).start()
         query_terms = lax.dot_general(delta_buf[...], key_rows[...], rows_first, preferred_element_type=F32)
         grad_rows[span, :] = query_terms.astype(BF16)
-        return carry
-
-    lax.fori_loop(0, QBLOCKS, block, 0, unroll=True)
-    for shift, result in enumerate(results):
-        target = (plane + shift) % PLANES
-        for owner in range(CORES):
-            span = pl.ds(pl.multiple_of((target * CORES + owner) * PIECE, 16), PIECE)
-            result[owner] = grad_rows[span, :]
+
+    states = [first(0)]
+    for step in range(QBLOCKS):
+        if step + 1 < QBLOCKS:
+            states.append(first(step + 1))
+        second(step, states[step])
+    spread(grad_rows, results)
 
     def finish(step, carry):
         for s in range(SELECTED):
@@ -233,63 +279,48 @@
     lax.fori_loop(0, QBLOCKS, finish, 0)
 
 
-def attend_backward(slots, packed, fetched, parcels):
+def attend_backward(slots, packed, fetched, queries, grads):
     rows = pltpu.VMEM((QBLOCKS * ROWS, HEAD_DIM), BF16)
     return pl.pallas_call(
         attend_kernel,
-        out_shape=(array(CTX, 2, BLOCK, HEAD_DIM),) + (array(CORES, PIECE, HEAD_DIM),) * PLANES,
-        in_specs=[IN_SMEM, IN_HBM, IN_VMEM] + [IN_VMEM] * PLANES,
-        out_specs=(IN_HBM,) + (IN_VMEM,) * PLANES,
+        out_shape=(array(CTX, 2, BLOCK, HEAD_DIM),) + (array(2, CORES, PIECE, HEAD_DIM),) * PAIRS,
+        in_specs=[IN_SMEM, IN_HBM, IN_VMEM, IN_VMEM, IN_VMEM],
+        out_specs=(IN_HBM,) + (IN_VMEM,) * PAIRS,
         scratch_shapes=[
+            pltpu.VMEM((QBLOCKS, KEYS, HEAD_DIM), BF16),
+            pltpu.VMEM((QBLOCKS, KEYS, HEAD_DIM), BF16),
             rows,
-            rows,
-            pltpu.VMEM((KEYS, HEAD_DIM), BF16),
-            pltpu.VMEM((KEYS, HEAD_DIM), BF16),
-            rows,
-            pltpu.VMEM((KEYS, ROWS), F32),
-            pltpu.VMEM((KEYS, ROWS), F32),
-            pltpu.VMEM((KEYS, ROWS), BF16),
+            pltpu.VMEM((QBLOCKS, KEYS, ROWS), F32),
+            pltpu.VMEM((QBLOCKS, KEYS, ROWS), F32),
+            pltpu.VMEM((QBLOCKS, KEYS, ROWS), BF16),
             pltpu.VMEM((QBLOCKS * SELECTED, 2, BLOCK, HEAD_DIM), BF16),
             pltpu.SemaphoreType.DMA((QBLOCKS * SELECTED,)),
         ],
         input_output_aliases={1: 0},
         compiler_params=pltpu.CompilerParams(vmem_limit_bytes=VMEM_ATTEND),
         name="attend_backward",
-    )(slots, packed, fetched, *parcels)
-
-
-def swap_kernel(*refs):
-    parcels, (keep, send) = refs[:PLANES], refs[PLANES:]
-    core = lax.axis_index("head") % CORES
-    for shift, parcel in enumerate(parcels):
-        keep[shift] = parcel[core]
-        send[shift] = parcel[1 - core]
-
-
-def swap(parcels):
-    out = array(PLANES, PIECE, HEAD_DIM)
-    return pl.pallas_call(
-        swap_kernel,
-        out_shape=(out, out),
-        in_specs=[IN_VMEM] * PLANES,
-        out_specs=(IN_VMEM, IN_VMEM),
-        compiler_params=pltpu.CompilerParams(vmem_limit_bytes=VMEM_LIMIT),
-        name="swap_cores",
-    )(*parcels)
+    )(slots, packed, fetched, queries, grads)
+
+
+def swap_kernel(near, far, keep, send):
+    core = position()[2]
+    for other, parcels in enumerate((near, far)):
+        for shift in range(PAIRS):
+            keep[other * PAIRS + shift] = parcels[shift, core]
+            send[other * PAIRS + shift] = parcels[shift, 1 - core]
 
 
 def merge_kernel(keep, got, query_grad):
-    head = lax.axis_index("head")
-    plane, core = head // CORES, head % CORES
+    pair, low_bit, core = position()
     shape = (TOKENS // 2, 8, HEAD_DIM)
     even, odd = [], []
     for source in range(PLANES):
-        shift = (plane - source + PLANES) % PLANES
+        shift = (source % 2 + low_bit) % 2 * PAIRS + (pair - source // 2 + PAIRS) % PAIRS
         mine = keep[shift].astype(F32).reshape(shape)
         other = got[shift].astype(F32).reshape(shape)
-        pair = halves(jnp.where(core == 0, mine, other), jnp.where(core == 0, other, mine))
-        even.append(pair[0])
-        odd.append(pair[1])
+        joined = halves(jnp.where(core == 0, mine, other), jnp.where(core == 0, other, mine))
+        even.append(joined[0])
+        odd.append(joined[1])
     both = jnp.stack([jnp.stack(even, 1), jnp.stack(odd, 1)], 1)
     query_grad[...] = both.reshape(TOKENS, PLANES * 8, HEAD_DIM).astype(BF16)
 
@@ -305,19 +336,21 @@
     )(keep, got)
 
 
-def sum_kernel(rows, terms, key_grad, value_grad, sums, halves_out, sems):
+def sum_kernel(rows_in, terms, key_grad, value_grad, sums, halves_out, rows, sems, row_sem):
+    fetch = pltpu.make_async_copy(rows_in, rows, row_sem)
+    fetch.start()
     sums[...] = jnp.zeros_like(sums)
-
-    def add(index, carry):
-        row = wanted_row(rows, index)
-        row = jnp.where(row < 0, OWNED, row)
-        for kind in range(2):
-            sums[kind, row] += terms[index, kind].astype(F32)
-        return carry
-
-    lax.fori_loop(0, CTX, add, 0, unroll=4)
+    fetch.wait()
     copies = []
     for kind, out in enumerate((key_grad, value_grad)):
+
+        def add(index, carry):
+            row = wanted_row(rows, index)
+            row = jnp.where(row < 0, OWNED, row)
+            sums[kind, row] += terms[index, kind].astype(F32)
+            return carry
+
+        lax.fori_loop(0, CTX, add, 0, unroll=8)
         for part in range(2):
             span = pl.ds(part * (OWNED // 2), OWNED // 2)
             halves_out[kind, span] = sums[kind, span].astype(BF16)
@@ -332,12 +365,14 @@
     return pl.pallas_call(
         sum_kernel,
         out_shape=(grad, grad),
-        in_specs=[IN_SMEM, IN_VMEM],
+        in_specs=[IN_HBM, IN_VMEM],
         out_specs=(IN_HBM, IN_HBM),
         scratch_shapes=[
             pltpu.VMEM((2, OWNED + 1, BLOCK, HEAD_DIM), F32),
             pltpu.VMEM((2, OWNED, BLOCK, HEAD_DIM), BF16),
+            pltpu.SMEM((1, QBLOCKS_ALL), jnp.int32),
             pltpu.SemaphoreType.DMA((2, 2)),
+            pltpu.SemaphoreType.DMA,
         ],
         compiler_params=pltpu.CompilerParams(vmem_limit_bytes=VMEM_LIMIT),
         name="owner_sum",
@@ -348,16 +383,31 @@
     return lax.all_to_all(blocks, "ctx", split_axis=0, concat_axis=0, tiled=True)
 
 
-def swap_partner(array):
-    return lax.ppermute(array, "head", [(i, i ^ 1) for i in range(PLANES * CORES)])
-
-
-def along_planes(parcels):
+def swap_bit(block, bit):
+    return lax.ppermute(block, "head", [(i, i ^ bit) for i in range(PLANES * CORES)])
+
+
+def along_pairs(parcels):
     moved = [parcels[0]]
-    for shift in range(1, PLANES):
-        pairs = [(i, (i + shift * CORES) % (PLANES * CORES)) for i in range(PLANES * CORES)]
+    for shift in range(1, PAIRS):
+        pairs = [(i, (i + shift * 2 * CORES) % (PLANES * CORES)) for i in range(PLANES * CORES)]
         moved.append(lax.ppermute(parcels[shift], "head", pairs))
     return moved
+
+
+def deliver(keep, send):
+    half = array(PAIRS, 4, PIECE, HEAD_DIM)
+    near, far = local(join_kernel, (half, half), "join_parcels", keep, swap_bit(send, 1))
+    parcel = array(2, 4, PIECE, HEAD_DIM)
+    return along_pairs(local(link_kernel, (parcel,) * PAIRS, "link_parcels", near, swap_bit(far, CORES)))
+
+
+def send_back(results):
+    half = array(PAIRS, CORES, PIECE, HEAD_DIM)
+    near, far = local(part_kernel, (half, half), "part_parcels", *along_pairs(results))
+    out = array(PLANES, PIECE, HEAD_DIM)
+    keep, send = local(swap_kernel, (out, out), "swap_cores", near, swap_bit(far, CORES))
+    return merge(keep, swap_bit(send, 1))
 
 
 def per_device(queries, keys, values, out_grad, selected):
@@ -368,11 +418,10 @@
     packed, rows = pack(table, keys.reshape(blocks), values.reshape(blocks))
     fetched = exchange(packed)
     keep, send = split(rows, queries, out_grad)
-    parcels = along_planes(join(keep, swap_partner(send)))
-    terms, *results = attend_backward(slots, packed, fetched, parcels)
+    parcels = deliver(keep, send)
+    terms, *results = attend_backward(slots, packed, fetched, *assemble(parcels))
     back = exchange(terms)
-    keep, send = swap(along_planes(results))
-    query_grad = merge(keep, swap_partner(send))
+    query_grad = send_back(results)
     key_grad, value_grad = owner_sum(rows, back)
     return query_grad, key_grad.reshape(keys.shape), value_grad.reshape(values.shape)
 

time: 144 us -> 143 us (level)
  the two profiles are of different devices: /device:TPU:410 before, /device:TPU:538 now
where the time goes in v4:
time: 143 us
  waiting for transfers between devices  67.4 us (47%)
  starting transfers between devices  62.4 us (44%)
  Pallas kernels  12 us (8%)
    all_to_all x2, waiting for transfers between devices, exchange(): lax.all_to_all(blocks, 'ctx', split_axis=0, concat_axis=0, tiled=True)  48 us
    ppermute x6, starting transfers between devices, along_pairs(): moved.append(lax.ppermute(parcels[shift], 'head', pairs))  27 us
    all_to_all x2, starting transfers between devices, exchange(): lax.all_to_all(blocks, 'ctx', split_axis=0, concat_axis=0, tiled=True)  22.7 us
    ppermute x4, starting transfers between devices, swap_bit(): lax.ppermute(block, 'head', [(i, i ^ bit) for i in range(PLANES * CORES)])  12.7 us
    ppermute x4, waiting for transfers between devices, swap_bit(): lax.ppermute(block, 'head', [(i, i ^ bit) for i in range(PLANES * CORES)])  10.4 us
    ppermute x6, waiting for transfers between devices, along_pairs(): moved.append(lax.ppermute(parcels[shift], 'head', pairs))  8.95 us
    pallas_call x1, Pallas kernels, attend_backward(): pl.pallas_call(attend_kernel, out_shape=(array(CTX, 2, BLOCK, HEAD_DIM),)...  4.81 us
    pallas_call x1, Pallas kernels, pack(): pl.pallas_call(pack_kernel, out_shape=(array(CTX, 2, BLOCK, HEAD_DIM), ar...  3.34 us
  transfers between devices with their start and end apart: 12, of which 9 were waited for; matrix products, arithmetic and copies ran while one was open for 0% of the time, Pallas kernels for 1%

profile of v4, /device:TPU:538, one launch (start us, length us, event | category | flops | bytes accessed | tf_op | source)
XLA Modules:
  0.0 142.7 jit_solution(11643088031295557724)
XLA Ops:
  0.6 3.3 %pack_blocks.1 = (bf16[64,2,64,128]{3,2,1,0:T(8,128)(2,1)}, s32[1,192]{1,0:T(1,128)}) custom-call(s32[16,192]{1,0:T(8,128)} %bitcast.27, bf16[32,64,128]{2,1,0:T(8,128)(2,1)} %bitcast.25, bf16[32,64,128]{2,1,0:T(8,128)(2,1)} %bitcast.26), custom_call_target="tpu_custom_call" | custom-call | tf_op jit(solution)/shard_map/pack_blocks/pallas_call | solution.py:85
  4.0 0.0 copy-start
  4.0 0.0 copy-start.1
  4.0 0.0 copy-start.2
  4.0 0.0 copy-start.3
  4.0 13.5 %all-to-all-start = ((bf16[64,2,64,128]{3,2,1,0:T(8,128)(2,1)}), bf16[64,2,64,128]{3,2,1,0:T(8,128)(2,1)S(1)}, u32[]{:S(2)}, u32[]{:S(2)}) async-start(bf16[64,2,64,128]{3,2,1,0:T(8,128)(2,1)} %get-tuple-element.26.unused), calls=%async_computation | async-start | bytes 4194304 | tf_op jit(solution)/shard_map/all_to_all | solution.py:383
  17.6 0.0 copy-done
  17.6 0.0 copy-done.1
  17.6 0.0 copy-done.2
  17.6 0.7 split_heads.1
  18.3 1.9 %collective-permute-start = (bf16[8,2,48,128]{3,2,1,0:T(8,128)(2,1)S(1)}, bf16[8,2,48,128]{3,2,1,0:T(8,128)(2,1)S(1)}, u32[]{:S(2)}, u32[]{:S(2)}) collective-permute-start(bf16[8,2,48,128]{3,2,1,0:T(8,128)(2,1)S(1)} %get-tuple-element.29), channel_id=1, source_target_pairs={{0,1},{1,0},{2,3},{3,2},{4,5},{5,4},{6,7},{7,6},{8,9},{9,8},{10,11... | collective-permute-start | bytes 589832 | tf_op jit(solution)/shard_map/ppermute | solution.py:387
  20.2 1.4 collective-permute-done.got
  21.6 4.3 %collective-permute-start.1 = (bf16[4,4,48,128]{3,2,1,0:T(8,128)(2,1)S(1)}, bf16[4,4,48,128]{3,2,1,0:T(8,128)(2,1)S(1)}, u32[]{:S(2)}, u32[]{:S(2)}) collective-permute-start(bf16[4,4,48,128]{3,2,1,0:T(8,128)(2,1)S(1)} %get-tuple-element.31), channel_id=1, source_target_pairs={{0,2},{1,3},{2,0},{3,1},{4,6},{5,7},{6,4},{7,5},{8,10},{9,11},{10,... | collective-permute-start | bytes 589832 | tf_op jit(solution)/shard_map/ppermute | solution.py:387
  25.9 5.2 %collective-permute-done.1.far = bf16[4,4,48,128]{3,2,1,0:T(8,128)(2,1)S(1)} collective-permute-done((bf16[4,4,48,128]{3,2,1,0:T(8,128)(2,1)S(1)}, bf16[4,4,48,128]{3,2,1,0:T(8,128)(2,1)S(1)}, u32[]{:S(2)}, u32[]{:S(2)}) %collective-permute-start.1) | collective-permute-done | bytes 196640 | tf_op jit(solution)/shard_map/ppermute | solution.py:387
  31.2 6.1 %collective-permute-start.2 = (bf16[2,4,48,128]{3,2,1,0:T(8,128)(2,1)S(1)}, bf16[2,4,48,128]{3,2,1,0:T(8,128)(2,1)S(1)}, u32[]{:S(2)}, u32[]{:S(2)}) collective-permute-start(bf16[2,4,48,128]{3,2,1,0:T(8,128)(2,1)S(1)} %get-tuple-element.33), channel_id=1, source_target_pairs={{0,4},{1,5},{2,6},{3,7},{4,8},{5,9},{6,10},{7,11},{8,12},{9,13},{1... | collective-permute-start | bytes 294920 | tf_op jit(solution)/shard_map/ppermute | solution.py:394
  37.3 1.9 %collective-permute-start.3 = (bf16[2,4,48,128]{3,2,1,0:T(8,128)(2,1)S(1)}, bf16[2,4,48,128]{3,2,1,0:T(8,128)(2,1)S(1)}, u32[]{:S(2)}, u32[]{:S(2)}) collective-permute-start(bf16[2,4,48,128]{3,2,1,0:T(8,128)(2,1)S(1)} %get-tuple-element.34), channel_id=1, source_target_pairs={{0,8},{1,9},{2,10},{3,11},{4,12},{5,13},{6,14},{7,15},{8,0},{9,1},... | collective-permute-start | bytes 294920 | tf_op jit(solution)/shard_map/ppermute | solution.py:394
  39.2 5.5 %collective-permute-start.4 = (bf16[2,4,48,128]{3,2,1,0:T(8,128)(2,1)S(1)}, bf16[2,4,48,128]{3,2,1,0:T(8,128)(2,1)S(1)}, u32[]{:S(2)}, u32[]{:S(2)}) collective-permute-start(bf16[2,4,48,128]{3,2,1,0:T(8,128)(2,1)S(1)} %get-tuple-element.35), channel_id=1, source_target_pairs={{0,12},{1,13},{2,14},{3,15},{4,0},{5,1},{6,2},{7,3},{8,4},{9,5},{1... | collective-permute-start | bytes 294920 | tf_op jit(solution)/shard_map/ppermute | solution.py:394
  44.7 0.0 copy-done.3
  44.7 0.1 add_select_fusion.slots
  44.8 0.0 collective-permute-done.2.refs_1_
  44.8 4.6 %collective-permute-done.3.refs_2_ = bf16[2,4,48,128]{3,2,1,0:T(8,128)(2,1)S(1)} collective-permute-done((bf16[2,4,48,128]{3,2,1,0:T(8,128)(2,1)S(1)}, bf16[2,4,48,128]{3,2,1,0:T(8,128)(2,1)S(1)}, u32[]{:S(2)}, u32[]{:S(2)}) %collective-permute-start.3) | collective-permute-done | bytes 98336 | tf_op jit(solution)/shard_map/ppermute | solution.py:394
  49.4 1.5 %collective-permute-done.4.refs_3_ = bf16[2,4,48,128]{3,2,1,0:T(8,128)(2,1)S(1)} collective-permute-done((bf16[2,4,48,128]{3,2,1,0:T(8,128)(2,1)S(1)}, bf16[2,4,48,128]{3,2,1,0:T(8,128)(2,1)S(1)}, u32[]{:S(2)}, u32[]{:S(2)}) %collective-permute-start.4) | collective-permute-done | bytes 98336 | tf_op jit(solution)/shard_map/ppermute | solution.py:394
  50.9 0.1 assemble_rows.1
  51.0 20.6 %all-to-all-done.fetched = bf16[64,2,64,128]{3,2,1,0:T(8,128)(2,1)S(1)} async-done(((bf16[64,2,64,128]{3,2,1,0:T(8,128)(2,1)}), bf16[64,2,64,128]{3,2,1,0:T(8,128)(2,1)S(1)}, u32[]{:S(2)}, u32[]{:S(2)}) %all-to-all-start) | async-done | bytes 2097184 | tf_op jit(solution)/shard_map/all_to_all | solution.py:383
  71.6 4.8 %attend_backward.1 = (bf16[64,2,64,128]{3,2,1,0:T(8,128)(2,1)}, bf16[2,2,48,128]{3,2,1,0:T(8,128)(2,1)S(1)}, bf16[2,2,48,128]{3,2,1,0:T(8,128)(2,1)S(1)}, bf16[2...) custom-call(s32[16,3]{1,0:T(8,128)S(1)} %add_select_fusion.slots, ...), custom_call_target="tpu_custom_call", output_to_operand_aliasing={{0}: (1, {})} | custom-call | tf_op jit(solution)/shard_map/attend_backward/pallas_call | solution.py:284
  76.4 9.2 %all-to-all-start.1 = ((bf16[64,2,64,128]{3,2,1,0:T(8,128)(2,1)}), bf16[64,2,64,128]{3,2,1,0:T(8,128)(2,1)S(1)}, u32[]{:S(2)}, u32[]{:S(2)}) async-start(bf16[64,2,64,128]{3,2,1,0:T(8,128)(2,1)} %get-tuple-element.46), calls=%async_computation.1 | async-start | bytes 4194304 | tf_op jit(solution)/shard_map/all_to_all | solution.py:383
  85.6 6.1 %collective-permute-start.5 = (bf16[2,2,48,128]{3,2,1,0:T(8,128)(2,1)S(1)}, bf16[2,2,48,128]{3,2,1,0:T(8,128)(2,1)S(1)}, u32[]{:S(2)}, u32[]{:S(2)}) collective-permute-start(bf16[2,2,48,128]{3,2,1,0:T(8,128)(2,1)S(1)} %get-tuple-element.39), channel_id=1, source_target_pairs={{0,4},{1,5},{2,6},{3,7},{4,8},{5,9},{6,10},{7,11},{8,12},{9,13},{1... | collective-permute-start | bytes 147464 | tf_op jit(solution)/shard_map/ppermute | solution.py:394
  91.7 1.9 %collective-permute-start.6 = (bf16[2,2,48,128]{3,2,1,0:T(8,128)(2,1)S(1)}, bf16[2,2,48,128]{3,2,1,0:T(8,128)(2,1)S(1)}, u32[]{:S(2)}, u32[]{:S(2)}) collective-permute-start(bf16[2,2,48,128]{3,2,1,0:T(8,128)(2,1)S(1)} %get-tuple-element.40), channel_id=1, source_target_pairs={{0,8},{1,9},{2,10},{3,11},{4,12},{5,13},{6,14},{7,15},{8,0},{9,1},... | collective-permute-start | bytes 147464 | tf_op jit(solution)/shard_map/ppermute | solution.py:394
  93.6 5.5 %collective-permute-start.7 = (bf16[2,2,48,128]{3,2,1,0:T(8,128)(2,1)S(1)}, bf16[2,2,48,128]{3,2,1,0:T(8,128)(2,1)S(1)}, u32[]{:S(2)}, u32[]{:S(2)}) collective-permute-start(bf16[2,2,48,128]{3,2,1,0:T(8,128)(2,1)S(1)} %get-tuple-element.41), channel_id=1, source_target_pairs={{0,12},{1,13},{2,14},{3,15},{4,0},{5,1},{6,2},{7,3},{8,4},{9,5},{1... | collective-permute-start | bytes 147464 | tf_op jit(solution)/shard_map/ppermute | solution.py:394
  99.1 0.0 collective-permute-done.5.refs_1_
  99.1 2.8 %collective-permute-done.6.refs_2_ = bf16[2,2,48,128]{3,2,1,0:T(8,128)(2,1)S(1)} collective-permute-done((bf16[2,2,48,128]{3,2,1,0:T(8,128)(2,1)S(1)}, bf16[2,2,48,128]{3,2,1,0:T(8,128)(2,1)S(1)}, u32[]{:S(2)}, u32[]{:S(2)}) %collective-permute-start.6) | collective-permute-done | bytes 49184 | tf_op jit(solution)/shard_map/ppermute | solution.py:394
  101.9 0.0 collective-permute-done.7.refs_3_
  102.0 4.5 %collective-permute-start.8 = (bf16[4,2,48,128]{3,2,1,0:T(8,128)(2,1)S(1)}, bf16[4,2,48,128]{3,2,1,0:T(8,128)(2,1)S(1)}, u32[]{:S(2)}, u32[]{:S(2)}) collective-permute-start(bf16[4,2,48,128]{3,2,1,0:T(8,128)(2,1)S(1)} %get-tuple-element.43), channel_id=1, source_target_pairs={{0,2},{1,3},{2,0},{3,1},{4,6},{5,7},{6,4},{7,5},{8,10},{9,11},{10,... | collective-permute-start | bytes 294920 | tf_op jit(solution)/shard_map/ppermute | solution.py:387
  106.5 2.6 %collective-permute-done.8.far = bf16[4,2,48,128]{3,2,1,0:T(8,128)(2,1)S(1)} collective-permute-done((bf16[4,2,48,128]{3,2,1,0:T(8,128)(2,1)S(1)}, bf16[4,2,48,128]{3,2,1,0:T(8,128)(2,1)S(1)}, u32[]{:S(2)}, u32[]{:S(2)}) %collective-permute-start.8) | collective-permute-done | bytes 98336 | tf_op jit(solution)/shard_map/ppermute | solution.py:387
  109.1 1.9 %collective-permute-start.9 = (bf16[8,48,128]{2,1,0:T(8,128)(2,1)S(1)}, bf16[8,48,128]{2,1,0:T(8,128)(2,1)S(1)}, u32[]{:S(2)}, u32[]{:S(2)}) collective-permute-start(bf16[8,48,128]{2,1,0:T(8,128)(2,1)S(1)} %get-tuple-element.45), channel_id=1, source_target_pairs={{0,1},{1,0},{2,3},{3,2},{4,5},{5,4},{6,7},{7,6},{8,9},{9,8},{10,11... | collective-permute-start | bytes 294920 | tf_op jit(solution)/shard_map/ppermute | solution.py:387
  111.0 1.3 collective-permute-done.9.got
  112.3 0.7 merge_heads.1
  113.0 27.4 %all-to-all-done.1.terms = bf16[64,2,64,128]{3,2,1,0:T(8,128)(2,1)S(1)} async-done(((bf16[64,2,64,128]{3,2,1,0:T(8,128)(2,1)}), bf16[64,2,64,128]{3,2,1,0:T(8,128)(2,1)S(1)}, u32[]{:S(2)}, u32[]{:S(2)}) %all-to-all-start.1) | async-done | bytes 2097184 | tf_op jit(solution)/shard_map/all_to_all | solution.py:383
  140.4 2.3 %owner_sum.1 = (bf16[32,64,128]{2,1,0:T(8,128)(2,1)}, bf16[32,64,128]{2,1,0:T(8,128)(2,1)}) custom-call(s32[1,192]{1,0:T(1,128)S(1)} %copy-done.2, bf16[64,2,64,128]{3,2,1,0:T(8,128)(2,1)S(1)} %all-to-all-done.1.terms), custom_call_target="tpu_custom_call" | custom-call | tf_op jit(solution)/shard_map/owner_sum/pallas_call | solution.py:365
  (4 shorter events, 0.1 us)
Async XLA Ops:
  4.0 13.6 %copy-start = (bf16[12,64,128]{2,1,0:T(8,128)(2,1)S(1)}, bf16[12,64,128]{2,1,0:T(8,128)(2,1)}, u32[]{:S(2)}) copy-start(bf16[12,64,128]{2,1,0:T(8,128)(2,1)} %queries.1) | copy-start | bytes 589828
  4.0 13.6 %copy-start.1 = (bf16[12,64,128]{2,1,0:T(8,128)(2,1)S(1)}, bf16[12,64,128]{2,1,0:T(8,128)(2,1)}, u32[]{:S(2)}) copy-start(bf16[12,64,128]{2,1,0:T(8,128)(2,1)} %grads.1) | copy-start | bytes 589828
  4.0 13.6 %copy-start.2 = (s32[1,192]{1,0:T(1,128)S(1)}, s32[1,192]{1,0:T(1,128)}, u32[]{:S(2)}) copy-start(s32[1,192]{1,0:T(1,128)} %get-tuple-element.27.rows.rows_in) | copy-start | bytes 2308
  4.0 40.7 %copy-start.3 = (s32[1,192,16]{1,2,0:T(8,128)S(1)}, s32[1,192,16]{1,2,0:T(8,128)}, u32[]{:S(2)}) copy-start(s32[1,192,16]{1,2,0:T(8,128)} %param.9) | copy-start | bytes 36868
  4.0 67.6 %all-to-all-start = ((bf16[64,2,64,128]{3,2,1,0:T(8,128)(2,1)}), bf16[64,2,64,128]{3,2,1,0:T(8,128)(2,1)S(1)}, u32[]{:S(2)}, u32[]{:S(2)}) async-start(bf16[64,2,64,128]{3,2,1,0:T(8,128)(2,1)} %get-tuple-element.26.unused), calls=%async_computation | async-start | bytes 4194304 | tf_op jit(solution)/shard_map/all_to_all | solution.py:383
  18.3 3.3 %collective-permute-start = (bf16[8,2,48,128]{3,2,1,0:T(8,128)(2,1)S(1)}, bf16[8,2,48,128]{3,2,1,0:T(8,128)(2,1)S(1)}, u32[]{:S(2)}, u32[]{:S(2)}) collective-permute-start(bf16[8,2,48,128]{3,2,1,0:T(8,128)(2,1)S(1)} %get-tuple-element.29), channel_id=1, source_target_pairs={{0,1},{1,0},{2,3},{3,2},{4,5},{5,4},{6,7},{7,6},{8,9},{9,8},{10,11... | collective-permute-start | bytes 589832 | tf_op jit(solution)/shard_map/ppermute | solution.py:387
  21.6 9.5 %collective-permute-start.1 = (bf16[4,4,48,128]{3,2,1,0:T(8,128)(2,1)S(1)}, bf16[4,4,48,128]{3,2,1,0:T(8,128)(2,1)S(1)}, u32[]{:S(2)}, u32[]{:S(2)}) collective-permute-start(bf16[4,4,48,128]{3,2,1,0:T(8,128)(2,1)S(1)} %get-tuple-element.31), channel_id=1, source_target_pairs={{0,2},{1,3},{2,0},{3,1},{4,6},{5,7},{6,4},{7,5},{8,10},{9,11},{10,... | collective-permute-start | bytes 589832 | tf_op jit(solution)/shard_map/ppermute | solution.py:387
  31.2 13.6 %collective-permute-start.2 = (bf16[2,4,48,128]{3,2,1,0:T(8,128)(2,1)S(1)}, bf16[2,4,48,128]{3,2,1,0:T(8,128)(2,1)S(1)}, u32[]{:S(2)}, u32[]{:S(2)}) collective-permute-start(bf16[2,4,48,128]{3,2,1,0:T(8,128)(2,1)S(1)} %get-tuple-element.33), channel_id=1, source_target_pairs={{0,4},{1,5},{2,6},{3,7},{4,8},{5,9},{6,10},{7,11},{8,12},{9,13},{1... | collective-permute-start | bytes 294920 | tf_op jit(solution)/shard_map/ppermute | solution.py:394
  37.3 12.1 %collective-permute-start.3 = (bf16[2,4,48,128]{3,2,1,0:T(8,128)(2,1)S(1)}, bf16[2,4,48,128]{3,2,1,0:T(8,128)(2,1)S(1)}, u32[]{:S(2)}, u32[]{:S(2)}) collective-permute-start(bf16[2,4,48,128]{3,2,1,0:T(8,128)(2,1)S(1)} %get-tuple-element.34), channel_id=1, source_target_pairs={{0,8},{1,9},{2,10},{3,11},{4,12},{5,13},{6,14},{7,15},{8,0},{9,1},... | collective-permute-start | bytes 294920 | tf_op jit(solution)/shard_map/ppermute | solution.py:394
  39.2 11.7 %collective-permute-start.4 = (bf16[2,4,48,128]{3,2,1,0:T(8,128)(2,1)S(1)}, bf16[2,4,48,128]{3,2,1,0:T(8,128)(2,1)S(1)}, u32[]{:S(2)}, u32[]{:S(2)}) collective-permute-start(bf16[2,4,48,128]{3,2,1,0:T(8,128)(2,1)S(1)} %get-tuple-element.35), channel_id=1, source_target_pairs={{0,12},{1,13},{2,14},{3,15},{4,0},{5,1},{6,2},{7,3},{8,4},{9,5},{1... | collective-permute-start | bytes 294920 | tf_op jit(solution)/shard_map/ppermute | solution.py:394
  76.4 64.0 %all-to-all-start.1 = ((bf16[64,2,64,128]{3,2,1,0:T(8,128)(2,1)}), bf16[64,2,64,128]{3,2,1,0:T(8,128)(2,1)S(1)}, u32[]{:S(2)}, u32[]{:S(2)}) async-start(bf16[64,2,64,128]{3,2,1,0:T(8,128)(2,1)} %get-tuple-element.46), calls=%async_computation.1 | async-start | bytes 4194304 | tf_op jit(solution)/shard_map/all_to_all | solution.py:383
  85.6 13.5 %collective-permute-start.5 = (bf16[2,2,48,128]{3,2,1,0:T(8,128)(2,1)S(1)}, bf16[2,2,48,128]{3,2,1,0:T(8,128)(2,1)S(1)}, u32[]{:S(2)}, u32[]{:S(2)}) collective-permute-start(bf16[2,2,48,128]{3,2,1,0:T(8,128)(2,1)S(1)} %get-tuple-element.39), channel_id=1, source_target_pairs={{0,4},{1,5},{2,6},{3,7},{4,8},{5,9},{6,10},{7,11},{8,12},{9,13},{1... | collective-permute-start | bytes 147464 | tf_op jit(solution)/shard_map/ppermute | solution.py:394
  91.7 10.2 %collective-permute-start.6 = (bf16[2,2,48,128]{3,2,1,0:T(8,128)(2,1)S(1)}, bf16[2,2,48,128]{3,2,1,0:T(8,128)(2,1)S(1)}, u32[]{:S(2)}, u32[]{:S(2)}) collective-permute-start(bf16[2,2,48,128]{3,2,1,0:T(8,128)(2,1)S(1)} %get-tuple-element.40), channel_id=1, source_target_pairs={{0,8},{1,9},{2,10},{3,11},{4,12},{5,13},{6,14},{7,15},{8,0},{9,1},... | collective-permute-start | bytes 147464 | tf_op jit(solution)/shard_map/ppermute | solution.py:394
  93.6 8.3 %collective-permute-start.7 = (bf16[2,2,48,128]{3,2,1,0:T(8,128)(2,1)S(1)}, bf16[2,2,48,128]{3,2,1,0:T(8,128)(2,1)S(1)}, u32[]{:S(2)}, u32[]{:S(2)}) collective-permute-start(bf16[2,2,48,128]{3,2,1,0:T(8,128)(2,1)S(1)} %get-tuple-element.41), channel_id=1, source_target_pairs={{0,12},{1,13},{2,14},{3,15},{4,0},{5,1},{6,2},{7,3},{8,4},{9,5},{1... | collective-permute-start | bytes 147464 | tf_op jit(solution)/shard_map/ppermute | solution.py:394
  102.0 7.1 %collective-permute-start.8 = (bf16[4,2,48,128]{3,2,1,0:T(8,128)(2,1)S(1)}, bf16[4,2,48,128]{3,2,1,0:T(8,128)(2,1)S(1)}, u32[]{:S(2)}, u32[]{:S(2)}) collective-permute-start(bf16[4,2,48,128]{3,2,1,0:T(8,128)(2,1)S(1)} %get-tuple-element.43), channel_id=1, source_target_pairs={{0,2},{1,3},{2,0},{3,1},{4,6},{5,7},{6,4},{7,5},{8,10},{9,11},{10,... | collective-permute-start | bytes 294920 | tf_op jit(solution)/shard_map/ppermute | solution.py:387
  109.1 3.2 %collective-permute-start.9 = (bf16[8,48,128]{2,1,0:T(8,128)(2,1)S(1)}, bf16[8,48,128]{2,1,0:T(8,128)(2,1)S(1)}, u32[]{:S(2)}, u32[]{:S(2)}) collective-permute-start(bf16[8,48,128]{2,1,0:T(8,128)(2,1)S(1)} %get-tuple-element.45), channel_id=1, source_target_pairs={{0,1},{1,0},{2,3},{3,2},{4,5},{5,4},{6,7},{7,6},{8,9},{9,8},{10,11... | collective-permute-start | bytes 294920 | tf_op jit(solution)/shard_map/ppermute | solution.py:387
